TPU v7x, 128 devices: a whole 4x4x4 slice. The times are simulated.
128 devices in a mesh: ctx: 16 (over y_lo, x, core), fsdp: 8 (over y_hi, z).
Axes of the slice: x: 4, y: 4 (y_hi: 2, y_lo: 2; y = y_hi * 2 + y_lo), z: 4, core: 2. Of those that a mesh axis runs over, the one named last changes fastest.
Arguments:
- inputs: bfloat16 [8, 2048, 960], P('fsdp', 'ctx'), may hold values from -6 to 6
- doc_offsets: int32 [8, 5], P('fsdp'), may hold values from 0 to 2048, as said below
- attn_gain: float32 [960], replicated, may hold values from 0.1 to 1.9
- query_weight: bfloat16 [960, 960], P('fsdp', 'ctx'), may hold values from -0.1875 to 0.1875
- key_weight: bfloat16 [960, 320], P('fsdp', 'ctx'), may hold values from -0.1875 to 0.1875
- value_weight: bfloat16 [960, 320], P('fsdp', 'ctx'), may hold values from -0.1875 to 0.1875
- proj_weight: bfloat16 [960, 960], P('fsdp', 'ctx'), may hold values from -3.5 to 3.5
- ffn_gain: float32 [960], replicated, may hold values from 0.1 to 1.9
- gate_weight: bfloat16 [960, 2560], P('fsdp', 'ctx'), may hold values from -0.1875 to 0.1875
- up_weight: bfloat16 [960, 2560], P('fsdp', 'ctx'), may hold values from -0.1875 to 0.1875
- down_weight: bfloat16 [2560, 960], P('fsdp', 'ctx'), may hold values from -0.125 to 0.125
- cotangent: bfloat16 [8, 2048, 960], P('fsdp', 'ctx'), may hold values from -6 to 6
Outputs:
- layer_out: bfloat16 [8, 2048, 960], P('fsdp', 'ctx')
- input_grad: bfloat16 [8, 2048, 960], P('fsdp', 'ctx')
- attn_gain_grad: float32 [960], replicated
- query_grad: float32 [960, 960], P('fsdp', 'ctx')
- key_grad: float32 [960, 320], P('fsdp', 'ctx')
- value_grad: float32 [960, 320], P('fsdp', 'ctx')
- proj_grad: float32 [960, 960], P('fsdp', 'ctx')
- ffn_gain_grad: float32 [960], replicated
- gate_grad: float32 [960, 2560], P('fsdp', 'ctx')
- up_grad: float32 [960, 2560], P('fsdp', 'ctx')
- down_grad: float32 [2560, 960], P('fsdp', 'ctx')
Inputs may be any that keep to these rules, and one draw needn't show every extreme that they name: `doc_offsets`: per sequence, 5 strictly rising offsets, the first 0 and the last 2048; consecutive ones bound a document.
All inputs are finite; a program needn't handle non-finite values.
Results may differ from a plain program's by a relative error of at most 0.025.
Values may be sent and summed in bfloat16 or wider, within the bound.
A program may use at most 128 MiB of HBM per device.

v0:
```python
import jax
import jax.numpy as jnp
from jax import lax
from jax.sharding import PartitionSpec as P

HEADS = 15
KVH = 5
HD = 64
NDOC = 4
QW = 960
KVW = 320


epsilon = 1e-05
block_rows = 512
masked_score = -1e30


def layout(offsets, token_index):
    inner = offsets[1:NDOC]
    after = token_index[:, None] >= inner[None, :]
    segment = jnp.sum(after.astype(jnp.int32), axis=1)
    starts = jnp.max(jnp.where(after, inner[None, :], 0), axis=1)
    return (segment, token_index - starts)


def rotary(positions):
    half_dim = HD // 2
    rate_table = 10000.0 ** (-2.0 * jnp.arange(half_dim, dtype=jnp.float32) / HD)
    angles = positions.astype(jnp.float32)[:, None] * rate_table[None, :]
    cosine = jnp.cos(angles)
    sine_table = jnp.sin(angles)
    return (
        jnp.concatenate([cosine, cosine], axis=1),
        jnp.concatenate([sine_table, sine_table], axis=1),
    )


def turn_half(vectors):
    half_dim = HD // 2
    return jnp.concatenate([-vectors[..., half_dim:], vectors[..., :half_dim]], axis=-1)


def rotate(vectors, cosine, sine_table):
    return vectors * cosine[:, None, :] + turn_half(vectors) * sine_table[:, None, :]


def unrotate(vectors, cosine, sine_table):
    return vectors * cosine[:, None, :] - turn_half(vectors) * sine_table[:, None, :]


def inner_rows(left, right):
    return lax.dot_general(
        left, right, (((0,), (0,)), ((), ())), preferred_element_type=jnp.float32
    )


def times_transposed(left, right):
    return lax.dot_general(
        left, right, (((1,), (1,)), ((), ())), preferred_element_type=jnp.float32
    )


def gather_weights(
    query_weight, key_weight, value_weight, proj_weight, gate_weight, up_weight, down_weight
):
    section = (
        lax.all_gather(query_weight, "fsdp", axis=0, tiled=True),
        lax.all_gather(key_weight, "fsdp", axis=0, tiled=True),
        lax.all_gather(value_weight, "fsdp", axis=0, tiled=True),
        lax.all_gather(proj_weight, "fsdp", axis=0, tiled=True),
        lax.all_gather(gate_weight, "fsdp", axis=0, tiled=True),
        lax.all_gather(up_weight, "fsdp", axis=0, tiled=True),
        lax.all_gather(down_weight, "fsdp", axis=0, tiled=True),
    )
    return (
        lax.all_gather(section[0], "ctx", axis=1, tiled=True),
        lax.all_gather(section[1], "ctx", axis=1, tiled=True),
        lax.all_gather(section[2], "ctx", axis=1, tiled=True),
        lax.all_gather(section[3], "ctx", axis=1, tiled=True),
        lax.all_gather(section[4], "ctx", axis=1, tiled=True),
        lax.all_gather(section[5], "ctx", axis=1, tiled=True),
        lax.all_gather(section[6], "ctx", axis=1, tiled=True),
    )


def reduce_grads(terms):
    section = (
        lax.psum_scatter(
            terms[0].astype(jnp.bfloat16), "ctx", scatter_dimension=1, tiled=True
        ).astype(jnp.float32),
        lax.psum_scatter(
            terms[1].astype(jnp.bfloat16), "ctx", scatter_dimension=1, tiled=True
        ).astype(jnp.float32),
        lax.psum_scatter(
            terms[2].astype(jnp.bfloat16), "ctx", scatter_dimension=1, tiled=True
        ).astype(jnp.float32),
        lax.psum_scatter(
            terms[3].astype(jnp.bfloat16), "ctx", scatter_dimension=1, tiled=True
        ).astype(jnp.float32),
        lax.psum_scatter(
            terms[4].astype(jnp.bfloat16), "ctx", scatter_dimension=1, tiled=True
        ).astype(jnp.float32),
        lax.psum_scatter(
            terms[5].astype(jnp.bfloat16), "ctx", scatter_dimension=1, tiled=True
        ).astype(jnp.float32),
        lax.psum_scatter(
            terms[6].astype(jnp.bfloat16), "ctx", scatter_dimension=1, tiled=True
        ).astype(jnp.float32),
    )
    return (
        lax.psum_scatter(
            section[0].astype(jnp.bfloat16), "fsdp", scatter_dimension=0, tiled=True
        ).astype(jnp.float32),
        lax.psum_scatter(
            section[1].astype(jnp.bfloat16), "fsdp", scatter_dimension=0, tiled=True
        ).astype(jnp.float32),
        lax.psum_scatter(
            section[2].astype(jnp.bfloat16), "fsdp", scatter_dimension=0, tiled=True
        ).astype(jnp.float32),
        lax.psum_scatter(
            section[3].astype(jnp.bfloat16), "fsdp", scatter_dimension=0, tiled=True
        ).astype(jnp.float32),
        lax.psum_scatter(
            section[4].astype(jnp.bfloat16), "fsdp", scatter_dimension=0, tiled=True
        ).astype(jnp.float32),
        lax.psum_scatter(
            section[5].astype(jnp.bfloat16), "fsdp", scatter_dimension=0, tiled=True
        ).astype(jnp.float32),
        lax.psum_scatter(
            section[6].astype(jnp.bfloat16), "fsdp", scatter_dimension=0, tiled=True
        ).astype(jnp.float32),
    )


def per_device(
    inputs,
    doc_offsets,
    attn_gain,
    query_weight,
    key_weight,
    value_weight,
    proj_weight,
    ffn_gain,
    gate_weight,
    up_weight,
    down_weight,
    cotangent,
):
    row_count = inputs.shape[1]
    length = row_count * lax.axis_size("ctx")
    group_size = HEADS // KVH
    score_scale = HD ** (-0.5)
    first_row = lax.axis_index("ctx") * row_count
    last_row = first_row + row_count - 1
    offsets = doc_offsets[0]
    token_index = first_row + jnp.arange(row_count, dtype=jnp.int32)
    segment, positions = layout(offsets, token_index)
    cosine, sine_table = rotary(positions)
    tokens = inputs[0].astype(jnp.float32)
    wide_query, wide_key, wide_value, wide_proj, wide_gate, wide_up, wide_down = gather_weights(
        query_weight, key_weight, value_weight, proj_weight, gate_weight, up_weight, down_weight
    )
    attn_scale = lax.rsqrt(jnp.mean(tokens * tokens, axis=-1, keepdims=True) + epsilon)
    normed = (tokens * attn_scale * attn_gain).astype(jnp.bfloat16)
    queries = jnp.dot(normed, wide_query, preferred_element_type=jnp.float32)
    keys_flat = jnp.dot(normed, wide_key, preferred_element_type=jnp.float32)
    value_rows = (
        jnp.dot(normed, wide_value, preferred_element_type=jnp.float32)
        .astype(jnp.bfloat16)
        .reshape(row_count, KVH, HD)
    )
    query_rot = (
        rotate(queries.reshape(row_count, HEADS, HD), cosine, sine_table)
        .astype(jnp.bfloat16)
        .reshape(row_count, KVH, group_size, HD)
    )
    key_rot = rotate(keys_flat.reshape(row_count, KVH, HD), cosine, sine_table).astype(jnp.bfloat16)

    def block_scores(key_block, key_start):
        key_index = key_start + jnp.arange(key_block.shape[0], dtype=jnp.int32)
        key_segment = layout(offsets, key_index)[0]
        allowed = (segment[:, None] == key_segment[None, :]) & (
            key_index[None, :] <= token_index[:, None]
        )
        scores = (
            jnp.einsum("qhgd,khd->hgqk", query_rot, key_block, preferred_element_type=jnp.float32)
            * score_scale
        )
        return jnp.where(allowed[None, None], scores, masked_score)

    def visit(carried, key_block, value_block, key_start):

        def update(current):
            row_top, row_total, weighted = current
            scores = block_scores(key_block, key_start)
            new_top = jnp.maximum(row_top, jnp.max(scores, axis=-1))
            factor = jnp.exp(row_top - new_top)
            raised = jnp.exp(scores - new_top[..., None])
            new_total = row_total * factor + jnp.sum(raised, axis=-1)
            added = jnp.einsum(
                "hgqk,khd->qhgd",
                raised.astype(jnp.bfloat16),
                value_block,
                preferred_element_type=jnp.float32,
            )
            return (
                new_top,
                new_total,
                weighted * jnp.transpose(factor, (2, 0, 1))[..., None] + added,
            )

        return lax.cond(key_start <= last_row, update, lambda current: current, carried)

    initial = (
        jnp.full((KVH, group_size, row_count), masked_score, jnp.float32),
        jnp.zeros((KVH, group_size, row_count), jnp.float32),
        jnp.zeros((row_count, KVH, group_size, HD), jnp.float32),
    )
    key_block = lax.all_gather(key_rot, "ctx", axis=0, tiled=True)
    value_block = lax.all_gather(value_rows, "ctx", axis=0, tiled=True)
    key_count = key_block.shape[0]
    steps_count = key_count // block_rows

    def scan_step(current, element):
        return (visit(current, element[0], element[1], element[2] * block_rows), None)

    row_top, row_total, weighted = lax.scan(
        scan_step,
        initial,
        (
            key_block.reshape(steps_count, block_rows, KVH, HD),
            value_block.reshape(steps_count, block_rows, KVH, HD),
            jnp.arange(steps_count, dtype=jnp.int32),
        ),
    )[0]
    log_total = row_top + jnp.log(row_total)
    mixed = weighted / jnp.transpose(row_total, (2, 0, 1))[..., None]
    attn_out = mixed.astype(jnp.bfloat16).reshape(row_count, QW)
    residual = tokens + jnp.dot(attn_out, wide_proj, preferred_element_type=jnp.float32)
    ffn_scale = lax.rsqrt(jnp.mean(residual * residual, axis=-1, keepdims=True) + epsilon)
    normed_ffn = (residual * ffn_scale * ffn_gain).astype(jnp.bfloat16)
    gate_value = jnp.dot(normed_ffn, wide_gate, preferred_element_type=jnp.float32)
    up_value = jnp.dot(normed_ffn, wide_up, preferred_element_type=jnp.float32)
    sigmoid_gate = jax.nn.sigmoid(gate_value)
    silu_gate = gate_value * sigmoid_gate
    hidden = (silu_gate * up_value).astype(jnp.bfloat16)
    layer_out = (residual + jnp.dot(hidden, wide_down, preferred_element_type=jnp.float32)).astype(
        jnp.bfloat16
    )
    wide_query, wide_key, wide_value, wide_proj, wide_gate, wide_up, wide_down = gather_weights(
        query_weight, key_weight, value_weight, proj_weight, gate_weight, up_weight, down_weight
    )
    cot_low = cotangent[0]
    down_term = inner_rows(hidden, cot_low)
    d_hidden = times_transposed(cot_low, wide_down)
    d_gate = (
        d_hidden * up_value * sigmoid_gate * (1.0 + gate_value * (1.0 - sigmoid_gate))
    ).astype(jnp.bfloat16)
    d_up = (d_hidden * silu_gate).astype(jnp.bfloat16)
    gate_term = inner_rows(normed_ffn, d_gate)
    up_term = inner_rows(normed_ffn, d_up)
    d_normed_ffn = times_transposed(d_gate, wide_gate) + times_transposed(d_up, wide_up)
    ffn_gain_term = jnp.sum(d_normed_ffn * residual * ffn_scale, axis=0)
    scaled_ffn = d_normed_ffn * ffn_gain
    d_residual = cot_low.astype(jnp.float32) + ffn_scale * (
        scaled_ffn
        - residual * ffn_scale * ffn_scale * jnp.mean(scaled_ffn * residual, axis=-1, keepdims=True)
    )
    d_branch = d_residual.astype(jnp.bfloat16)
    proj_term = inner_rows(attn_out, d_branch)
    d_mixed = (
        times_transposed(d_branch, wide_proj)
        .astype(jnp.bfloat16)
        .reshape(row_count, KVH, group_size, HD)
    )
    row_delta = jnp.transpose(jnp.sum(d_mixed.astype(jnp.float32) * mixed, axis=-1), (1, 2, 0))
    all_keys, all_values = (
        lax.all_gather(key_rot, "ctx", axis=0, tiled=True),
        lax.all_gather(value_rows, "ctx", axis=0, tiled=True),
    )
    key_block_rows = min(block_rows, length)
    block_count = length // key_block_rows
    empty_block = jnp.zeros((key_block_rows, KVW), jnp.float32)

    def backward_step(d_query, element):
        key_block, value_block, block_index = element
        key_start = block_index * key_block_rows

        def contribute(pending):
            shares = jnp.exp(block_scores(key_block, key_start) - log_total[..., None])
            d_shares = jnp.einsum(
                "qhgd,khd->hgqk", d_mixed, value_block, preferred_element_type=jnp.float32
            )
            d_scores = (shares * (d_shares - row_delta[..., None])).astype(jnp.bfloat16)
            d_query_add = (
                jnp.einsum(
                    "hgqk,khd->qhgd", d_scores, key_block, preferred_element_type=jnp.float32
                )
                * score_scale
            )
            d_key_block = (
                jnp.einsum(
                    "hgqk,qhgd->khd", d_scores, query_rot, preferred_element_type=jnp.float32
                )
                * score_scale
            )
            d_value_block = jnp.einsum(
                "hgqk,qhgd->khd",
                shares.astype(jnp.bfloat16),
                d_mixed,
                preferred_element_type=jnp.float32,
            )
            return (
                pending + d_query_add,
                d_key_block.reshape(key_block_rows, KVW),
                d_value_block.reshape(key_block_rows, KVW),
            )

        def skipped(pending):
            return (pending, empty_block, empty_block)

        d_query, d_key_block, d_value_block = lax.cond(
            key_start <= last_row, contribute, skipped, d_query
        )
        return (d_query, (d_key_block, d_value_block))

    d_query_rot, stacked = lax.scan(
        backward_step,
        jnp.zeros((row_count, KVH, group_size, HD), jnp.float32),
        (
            all_keys.reshape(block_count, key_block_rows, KVH, HD),
            all_values.reshape(block_count, key_block_rows, KVH, HD),
            jnp.arange(block_count, dtype=jnp.int32),
        ),
    )
    key_sums, value_sums = (
        lax.psum_scatter(
            stacked[0].reshape(length, KVW).astype(jnp.bfloat16),
            "ctx",
            scatter_dimension=0,
            tiled=True,
        ).astype(jnp.float32),
        lax.psum_scatter(
            stacked[1].reshape(length, KVW).astype(jnp.bfloat16),
            "ctx",
            scatter_dimension=0,
            tiled=True,
        ).astype(jnp.float32),
    )
    d_queries = (
        unrotate(d_query_rot.reshape(row_count, HEADS, HD), cosine, sine_table)
        .astype(jnp.bfloat16)
        .reshape(row_count, QW)
    )
    d_keys = (
        unrotate(key_sums.reshape(row_count, KVH, HD), cosine, sine_table)
        .astype(jnp.bfloat16)
        .reshape(row_count, KVW)
    )
    d_values = value_sums.astype(jnp.bfloat16)
    query_term = inner_rows(normed, d_queries)
    key_term = inner_rows(normed, d_keys)
    value_term = inner_rows(normed, d_values)
    d_normed = (
        times_transposed(d_queries, wide_query)
        + times_transposed(d_keys, wide_key)
        + times_transposed(d_values, wide_value)
    )
    attn_gain_term = jnp.sum(d_normed * tokens * attn_scale, axis=0)
    scaled_attn = d_normed * attn_gain
    d_tokens = d_residual + attn_scale * (
        scaled_attn
        - tokens * attn_scale * attn_scale * jnp.mean(scaled_attn * tokens, axis=-1, keepdims=True)
    )
    gain_totals = lax.psum((attn_gain_term, ffn_gain_term), ("ctx", "fsdp"))
    reduced = reduce_grads(
        (query_term, key_term, value_term, proj_term, gate_term, up_term, down_term)
    )
    return (
        layer_out[None],
        d_tokens.astype(jnp.bfloat16)[None],
        gain_totals[0],
        reduced[0],
        reduced[1],
        reduced[2],
        reduced[3],
        gain_totals[1],
        reduced[4],
        reduced[5],
        reduced[6],
    )


def solution(mesh):
    return jax.shard_map(
        per_device,
        mesh=mesh,
        in_specs=(
            P("fsdp", "ctx", None),
            P("fsdp", None),
            P(),
            P("fsdp", "ctx"),
            P("fsdp", "ctx"),
            P("fsdp", "ctx"),
            P("fsdp", "ctx"),
            P(),
            P("fsdp", "ctx"),
            P("fsdp", "ctx"),
            P("fsdp", "ctx"),
            P("fsdp", "ctx", None),
        ),
        out_specs=(
            P("fsdp", "ctx", None),
            P("fsdp", "ctx", None),
            P(),
            P("fsdp", "ctx"),
            P("fsdp", "ctx"),
            P("fsdp", "ctx"),
            P("fsdp", "ctx"),
            P(),
            P("fsdp", "ctx"),
            P("fsdp", "ctx"),
            P("fsdp", "ctx"),
        ),
        check_vma=False,
    )
```

profile of v0, /device:TPU:0, one launch (start us, length us, event | category | flops | bytes accessed | tf_op | source)
XLA Modules:
  0.0 1072.5 jit_solution(511170448785404448)
XLA Ops:
  9.4 36.1 %all-gather = bf16[8,120,20]{1,2,0:T(8,128)(2,1)S(1)} all-gather(bf16[1,120,20]{1,2,0:T(8,128)(2,1)} %bitcast.328), channel_id=1, replica_groups=mesh['ctx'=16,'fsdp'=8] {'fsdp'}, dimensions={0}, use_global_device_ids=true | all-gather | bytes 43200 | tf_op jit(solution)/shard_map/all_gather | solution.py:69
  45.6 20.9 %all-gather.1 = bf16[16,20,960]{2,1,0:T(8,128)(2,1)S(1)} all-gather(bf16[1,20,960]{2,1,0:T(8,128)(2,1)S(1)} %bitcast.319), channel_id=1, replica_groups=mesh['ctx'=16,'fsdp'=8] {'ctx'}, dimensions={0}, use_global_device_ids=true | all-gather | bytes 652800 | tf_op jit(solution)/shard_map/all_gather | solution.py:78
  68.1 34.4 %all-gather.4 = bf16[8,120,20]{1,2,0:T(8,128)(2,1)S(1)} all-gather(bf16[1,120,20]{1,2,0:T(8,128)(2,1)S(1)} %bitcast.329), channel_id=1, replica_groups=mesh['ctx'=16,'fsdp'=8] {'fsdp'}, dimensions={0}, use_global_device_ids=true | all-gather | bytes 43200 | tf_op jit(solution)/shard_map/all_gather | solution.py:70
  102.6 18.6 %all-gather.5 = bf16[16,20,960]{2,1,0:T(8,128)(2,1)S(1)} all-gather(bf16[1,20,960]{2,1,0:T(8,128)(2,1)S(1)} %bitcast.320), channel_id=1, replica_groups=mesh['ctx'=16,'fsdp'=8] {'ctx'}, dimensions={0}, use_global_device_ids=true | all-gather | bytes 652800 | tf_op jit(solution)/shard_map/all_gather | solution.py:79
  122.8 34.2 %all-gather.6 = bf16[8,120,60]{1,2,0:T(8,128)(2,1)S(1)} all-gather(bf16[1,120,60]{1,2,0:T(8,128)(2,1)S(1)} %bitcast.325), channel_id=1, replica_groups=mesh['ctx'=16,'fsdp'=8] {'fsdp'}, dimensions={0}, use_global_device_ids=true | all-gather | bytes 129600 | tf_op jit(solution)/shard_map/all_gather | solution.py:71
  157.9 34.2 %all-gather.2 = bf16[8,120,60]{1,2,0:T(8,128)(2,1)S(1)} all-gather(bf16[1,120,60]{1,2,0:T(8,128)(2,1)S(1)} %bitcast.326), channel_id=1, replica_groups=mesh['ctx'=16,'fsdp'=8] {'fsdp'}, dimensions={0}, use_global_device_ids=true | all-gather | bytes 129600 | tf_op jit(solution)/shard_map/all_gather | solution.py:68
  193.2 34.9 %all-gather.10 = bf16[8,320,60]{1,2,0:T(8,128)(2,1)S(1)} all-gather(bf16[1,320,60]{1,2,0:T(8,128)(2,1)S(1)} %bitcast.322), channel_id=1, replica_groups=mesh['ctx'=16,'fsdp'=8] {'fsdp'}, dimensions={0}, use_global_device_ids=true | all-gather | bytes 345600 | tf_op jit(solution)/shard_map/all_gather | solution.py:74
  229.4 35.5 %all-gather.9 = bf16[8,120,160]{1,2,0:T(8,128)(2,1)S(1)} all-gather(bf16[1,120,160]{1,2,0:T(8,128)(2,1)S(1)} %bitcast.323), channel_id=1, replica_groups=mesh['ctx'=16,'fsdp'=8] {'fsdp'}, dimensions={0}, use_global_device_ids=true | all-gather | bytes 345600 | tf_op jit(solution)/shard_map/all_gather | solution.py:73
  266.2 35.0 %all-gather.8 = bf16[8,120,160]{1,2,0:T(8,128)(2,1)S(1)} all-gather(bf16[1,120,160]{1,2,0:T(8,128)(2,1)S(1)} %bitcast.324), channel_id=1, replica_groups=mesh['ctx'=16,'fsdp'=8] {'fsdp'}, dimensions={0}, use_global_device_ids=true | all-gather | bytes 345600 | tf_op jit(solution)/shard_map/all_gather | solution.py:72
  302.5 1.5 copy.117
  304.0 2.6 copy.116
  306.6 4.0 reshape.330
  310.7 3.9 dot_general.102
  314.6 2.3 fusion.83
  317.2 9.3 while.33
  318.4 4.1 conditional.6
  319.6 2.1 fusion.18
  326.6 2.4 multiply_reduce_fusion.3
  329.3 7.7 reshape.338
  337.0 5.6 fusion.104
  342.6 11.8 %all-gather.24.cloned.1.call-done = bf16[960,2560]{0,1:T(8,128)(2,1)} async-done(((bf16[960,160]{0,1:T(8,128)(2,1)}), bf16[960,2560]{0,1:T(8,128)(2,1)}) %all-gather.24.cloned.1.call-update) | async-done | bytes 4915216 | tf_op jit(solution)/shard_map/all_gather | solution.py:81
  354.3 4.5 fusion.103
  358.9 5.1 multiply_convert_fusion
  364.0 2.2 fusion.105
  366.3 1.9 multiply_reduce_fusion
  370.2 15.2 %while.34 = (s32[]{:T(128)}, f32[128,5,3,64]{0,3,2,1:T(8,128)S(1)}, bf16[4,512,320]{1,2,0:T(8,128)(2,1)}, bf16[4,512,320]{1,2,0:T(8,128)(2,1)}, s32[4]{0:T(128)S...) while((s32[]{:T(128)}, f32[128,5,3,64]{0,3,2,1:T(8,128)S(1)}, ...), condition=%wide.region_17.18_spmd.clone, body=%wide.region_13.17_spmd.clone.sunk | while | flops 639750784 | bytes 23857592 | solution.py:328
  371.7 6.0 conditional.7
  374.1 2.3 fusion.32
  385.4 2.6 copy.108
  388.1 1.5 copy.109
  389.8 4.0 convolution_convert_fusion
  394.8 3.9 convolution_convert_fusion.1
  400.8 2.0 convolution_convert_fusion.3
  402.9 3.6 convolution_convert_fusion.2
  406.5 61.4 %reduce-scatter.36.cloned.1.call-done = bf16[128,320]{1,0:T(8,128)(2,1)} async-done(((bf16[2048,320]{1,0:T(8,128)(2,1)}), bf16[128,320]{1,0:T(8,128)(2,1)}) %reduce-scatter.36.cloned.1.call-update) | async-done | bytes 81936
  470.3 61.0 %reduce-scatter.38.cloned.1.call-done = bf16[128,320]{1,0:T(8,128)(2,1)} async-done(((bf16[2048,320]{1,0:T(8,128)(2,1)}), bf16[128,320]{1,0:T(8,128)(2,1)}) %reduce-scatter.38.cloned.1.call-update) | async-done | bytes 81936
  531.4 2.3 convolution_convert_fusion.5
  533.6 97.2 %fusion.102 = (bf16[960,64]{0,1:T(8,128)(2,1)S(1)}, bf16[960,64]{0,1:T(8,128)(2,1)}, bf16[960,24]{0,1:T(8,128)(2,1)}, bf16[960,24]{0,1:T(8,128)(2,1)S(1)}, bf16[2560,64]{0,1:T(8,128)(2,1)}) fusion(bf16[960,960]{0,1:T(8,128)(2,1)S(1)} %convolution_convert_fusion.4, bf16[960,960]{0,1:T(8,128)(2,1)} %convolution_convert_fusion.3, ...), kind=kCustom, calls=%all-reduce-scatter.5 | all-reduce-scatter fusion | flops 5324802 | bytes 10496512
  630.8 1.4 collective-permute-start.2
  632.2 1.5 collective-permute-start.1
  634.6 1.4 collective-permute-start.3
  637.3 7.9 collective-permute-start.5
  645.2 1.5 collective-permute-start.4
  648.7 2.4 collective-permute-start.6
  651.1 2.5 collective-permute-start.7
  653.6 2.6 collective-permute-start
  658.0 1.6 collective-permute-start.8
  663.8 4.3 concatenate.31
  668.1 1.9 constant_dynamic-slice_fusion
  670.1 2.1 copy.106
  672.2 2.2 reshape.318
  675.6 1.9 reshape.322
  677.5 1.8 fusion.78
  679.3 4.8 fusion.57
  684.2 2.1 copy.104
  686.4 1.5 fusion.106
  689.4 68.6 %all-reduce.14 = (f32[960]{0:T(1024)}, f32[960]{0:T(1024)}) all-reduce(f32[960]{0:T(1024)S(1)} %get-tuple-element.540, f32[960]{0:T(1024)S(1)} %get-tuple-element.538), channel_id=1, replica_groups=mesh['ctx'=16,'fsdp'=8] {'ctx','fsdp'}, use_global_device_ids=true, to_apply=%region_22.23 | all-reduce | flops 1920 | bytes 15360 | tf_op jit(solution)/shard_map/psum | solution.py:376
  758.0 2.0 copy.102
  760.9 4.3 all-reduce.21.cloned.1.call-done
  766.7 83.9 %all-reduce.23.cloned.1.call-done = (bf16[960,60]{0,1:T(8,128)(2,1)}, bf16[960,60]{0,1:T(8,128)(2,1)}) async-done(((bf16[960,60]{0,1:T(8,128)(2,1)}, bf16[960,60]{0,1:T(8,128)(2,1)}), (bf16[960,60]{0,1:T(8,128)(2,1)}, bf16[960,60]{0,1:T(8,128)(2,1)})) %all-reduce.23.cloned.1.call-update) | async-done | bytes 230416
  850.6 1.5 dynamic-slice_convert_fusion
  852.1 71.0 %reduce-scatter.44.cloned.1.call-done = bf16[320,60]{1,0:T(8,128)(2,1)} async-done(((bf16[2560,60]{1,0:T(8,128)(2,1)}), bf16[320,60]{1,0:T(8,128)(2,1)}) %reduce-scatter.44.cloned.1.call-update) | async-done | bytes 38416
  924.7 68.8 %reduce-scatter.42.cloned.1.call-done = bf16[120,160]{1,0:T(8,128)(2,1)} async-done(((bf16[960,160]{1,0:T(8,128)(2,1)}), bf16[120,160]{1,0:T(8,128)(2,1)}) %reduce-scatter.42.cloned.1.call-update) | async-done | bytes 38416
  995.1 68.8 %reduce-scatter.40.cloned.1.call-done = bf16[120,160]{1,0:T(8,128)(2,1)} async-done(((bf16[960,160]{1,0:T(8,128)(2,1)}), bf16[120,160]{1,0:T(8,128)(2,1)}) %reduce-scatter.40.cloned.1.call-update) | async-done | bytes 38416
  (281 shorter events, 52.2 us)
Async XLA Ops:
  7.2 59.7 %copy-start = (bf16[1,128,960]{1,2,0:T(8,128)(2,1)S(1)}, bf16[1,128,960]{1,2,0:T(8,128)(2,1)}, u32[]{:S(2)}) copy-start(bf16[1,128,960]{1,2,0:T(8,128)(2,1)} %param.20) | copy-start | bytes 737284
  7.2 59.7 %copy-start.30 = (f32[960]{0:T(1024)S(1)}, f32[960]{0:T(1024)}, u32[]{:S(2)}) copy-start(f32[960]{0:T(1024)} %param.22) | copy-start | bytes 11524
  7.2 295.3 %all-gather.20.cloned.1.call-start = ((), (), s32[]{:S(2)}) async-start(), calls=%async_computation.7 | async-start | bytes 1392640 | tf_op jit(solution)/shard_map/all_gather | solution.py:220
  45.6 22.5 %copy-start.38 = (bf16[120,20]{0,1:T(8,128)(2,1)S(1)}, bf16[120,20]{0,1:T(8,128)(2,1)}, u32[]{:S(2)}) copy-start(bf16[120,20]{0,1:T(8,128)(2,1)} %param.25) | copy-start | bytes 14404
  66.5 54.7 %copy-start.9 = (bf16[16,20,960]{2,1,0:T(8,128)(2,1)}, bf16[16,20,960]{2,1,0:T(8,128)(2,1)S(1)}, u32[]{:S(2)}) copy-start(bf16[16,20,960]{2,1,0:T(8,128)(2,1)S(1)} %all-gather.1) | copy-start | bytes 1843204
  67.3 55.4 %copy-start.35 = (bf16[120,60]{0,1:T(8,128)(2,1)S(1)}, bf16[120,60]{0,1:T(8,128)(2,1)}, u32[]{:S(2)}) copy-start(bf16[120,60]{0,1:T(8,128)(2,1)} %param.26) | copy-start | bytes 43204
  68.0 236.0 %all-gather.22.cloned.1.call-start = ((), (), s32[]{:S(2)}) async-start(), calls=%async_computation.8 | async-start | bytes 1392640 | tf_op jit(solution)/shard_map/all_gather | solution.py:221
  102.6 55.3 %copy-start.36 = (bf16[120,60]{0,1:T(8,128)(2,1)S(1)}, bf16[120,60]{0,1:T(8,128)(2,1)}, u32[]{:S(2)}) copy-start(bf16[120,60]{0,1:T(8,128)(2,1)} %param.23) | copy-start | bytes 43204
  121.3 71.9 %copy-start.31 = (bf16[320,60]{0,1:T(8,128)(2,1)S(1)}, bf16[320,60]{0,1:T(8,128)(2,1)}, u32[]{:S(2)}) copy-start(bf16[320,60]{0,1:T(8,128)(2,1)} %param.30) | copy-start | bytes 115204
  121.6 107.8 %copy-start.18 = (bf16[320,960]{1,0:T(8,128)(2,1)}, bf16[320,960]{1,0:T(8,128)(2,1)S(1)}, u32[]{:S(2)}) copy-start(bf16[320,960]{1,0:T(8,128)(2,1)S(1)} %reshape.326) | copy-start | bytes 1843204
  122.7 106.7 %copy-start.32 = (bf16[120,160]{0,1:T(8,128)(2,1)S(1)}, bf16[120,160]{0,1:T(8,128)(2,1)}, u32[]{:S(2)}) copy-start(bf16[120,160]{0,1:T(8,128)(2,1)} %param.29) | copy-start | bytes 115204
  122.7 183.9 %all-gather.30.cloned.1.call-start = ((), (), s32[]{:S(2)}) async-start(), calls=%async_computation.14 | async-start | bytes 2228224 | tf_op jit(solution)/shard_map/all_gather | solution.py:80
  157.9 152.8 %all-gather.28.cloned.1.call-start = ((), (), s32[]{:S(2)}) async-start(), calls=%async_computation.13 | async-start | bytes 2228224 | tf_op jit(solution)/shard_map/all_gather | solution.py:77
  193.1 136.1 %all-gather.32.cloned.1.call-start = ((), (), s32[]{:S(2)}) async-start(), calls=%async_computation.15 | async-start | bytes 5570560 | tf_op jit(solution)/shard_map/all_gather | solution.py:83
  193.2 73.0 %copy-start.33 = (bf16[120,160]{0,1:T(8,128)(2,1)S(1)}, bf16[120,160]{0,1:T(8,128)(2,1)}, u32[]{:S(2)}) copy-start(bf16[120,160]{0,1:T(8,128)(2,1)} %param.28) | copy-start | bytes 115204
  229.4 107.6 %all-gather.26.cloned.1.call-start = ((), (), s32[]{:S(2)}) async-start(), calls=%async_computation.10 | async-start | bytes 5570560 | tf_op jit(solution)/shard_map/all_gather | solution.py:82
  266.1 88.2 %all-gather.24.cloned.1.call-start = ((), (), s32[]{:S(2)}) async-start(), calls=%async_computation.9 | async-start | bytes 5570560 | tf_op jit(solution)/shard_map/all_gather | solution.py:81
  302.4 165.5 %reduce-scatter.36.cloned.1.call-start = ((), (), s32[]{:S(2)}) async-start(), calls=%async_computation.16 | async-start | bytes 1671168
  314.6 2.6 copy-start.40
  326.5 2.6 copy-start.10
  326.5 2.6 copy-start.34
  326.5 10.4 copy-start.20
  329.2 25.1 %copy-start.3 = (bf16[128,960]{0,1:T(8,128)(2,1)}, bf16[128,960]{0,1:T(8,128)(2,1)S(1)}, u32[]{:S(2)}) copy-start(bf16[128,960]{0,1:T(8,128)(2,1)S(1)} %multiply_convert_fusion.3) | copy-start | bytes 737284
  342.6 16.3 %copy-start.22 = (bf16[1,128,960]{1,2,0:T(8,128)(2,1)S(1)}, bf16[1,128,960]{1,2,0:T(8,128)(2,1)}, u32[]{:S(2)}) copy-start(bf16[1,128,960]{1,2,0:T(8,128)(2,1)} %param.31) | copy-start | bytes 737284
  354.3 9.7 slice-start.2
  354.3 11.9 %slice-start = ((s8[5242880]{0:T(1024)(128)(4,1)}), s8[4194304]{0:T(1024)(128)(4,1)S(1)}, s32[]{:S(2)}) async-start(s8[5242880]{0:T(1024)(128)(4,1)} %bitcast.297), calls=%async_computation.23 | async-start | bytes 8388608
  358.9 5.2 slice-start.3
  358.9 7.4 slice-start.1
  364.0 2.2 copy-start.14
  364.0 2.2 copy-start.16
  366.3 2.2 copy-start.1
  368.4 1.8 copy-start.6
  368.4 1.7 copy-start.41
  385.4 2.7 copy-start.24
  388.1 143.3 %reduce-scatter.38.cloned.1.call-start = ((), (), s32[]{:S(2)}) async-start(), calls=%async_computation.17 | async-start | bytes 1671168
  388.1 1.6 copy-start.4
  389.7 294.5 %reduce-scatter.34.cloned.1.call-start = ((), (), s32[]{:S(2)}) async-start(), calls=%async_computation.12 | async-start | bytes 5570560 | tf_op jit(solution)/shard_map/reduce_scatter | solution.py:104
  393.8 364.3 %reduce-scatter.32.cloned.1.call-start = ((), (), s32[]{:S(2)}) async-start(), calls=%async_computation.11 | async-start | bytes 5570560 | tf_op jit(solution)/shard_map/reduce_scatter | solution.py:101
  398.8 366.5 %all-reduce.21.cloned.1.call-start = ((), (), s32[]{:S(2)}) async-start(), calls=%async_computation.21 | async-start | bytes 196608
  399.8 3.1 copy-start.13
  399.8 3.0 copy-start.23
  533.6 102.4 %copy-start.39 = (u32[128]{0:T(128)S(1)}, u32[128]{0:T(128)}, u32[]{:S(2)}) copy-start(u32[128]{0:T(128)} %constant.121) | copy-start | bytes 1540
  630.8 30.0 %copy-start.25 = (bf16[960,64]{0,1:T(8,128)(2,1)S(1)}, bf16[960,64]{0,1:T(8,128)(2,1)}, u32[]{:S(2)}) copy-start(bf16[960,64]{0,1:T(8,128)(2,1)} %get-tuple-element.610) | copy-start | bytes 368644
  630.8 20.3 %collective-permute-start.2 = (bf16[960,24]{0,1:T(8,128)(2,1)}, bf16[960,24]{0,1:T(8,128)(2,1)S(1)}, u32[]{:S(2)}, u32[]{:S(2)}) collective-permute-start(bf16[960,24]{0,1:T(8,128)(2,1)} %get-tuple-element.611), channel_id=1, source_target_pairs={{0,16},{8,24},{16,32},{24,40},{32,48},{40,56},{48,64},{56,72},{64,... | collective-permute-start | bytes 138248
  632.2 21.3 %collective-permute-start.1 = (bf16[960,24]{0,1:T(8,128)(2,1)}, bf16[960,24]{0,1:T(8,128)(2,1)S(1)}, u32[]{:S(2)}, u32[]{:S(2)}) collective-permute-start(bf16[960,24]{0,1:T(8,128)(2,1)} %get-tuple-element.611), channel_id=1, source_target_pairs={{0,8},{8,16},{16,24},{24,32},{32,40},{40,48},{48,56},{56,64},{64,7... | collective-permute-start | bytes 138248
  634.6 29.3 %copy-start.12 = (bf16[2560,64]{0,1:T(8,128)(2,1)S(1)}, bf16[2560,64]{0,1:T(8,128)(2,1)}, u32[]{:S(2)}) copy-start(bf16[2560,64]{0,1:T(8,128)(2,1)} %get-tuple-element.613) | copy-start | bytes 983044
  634.6 14.1 %collective-permute-start.3 = (bf16[960,12]{0,1:T(8,128)(2,1)S(1)}, bf16[960,12]{0,1:T(8,128)(2,1)S(1)}, u32[]{:S(2)}, u32[]{:S(2)}) collective-permute-start(bf16[960,12]{0,1:T(8,128)(2,1)S(1)} %slice.56), channel_id=1, source_target_pairs={{0,24},{8,32},{16,40},{24,48},{32,56},{40,64},{48,72},{56,80},{64,... | collective-permute-start | bytes 69128
  637.3 22.3 %collective-permute-start.5 = (bf16[960,24]{0,1:T(8,128)(2,1)S(1)}, bf16[960,24]{0,1:T(8,128)(2,1)S(1)}, u32[]{:S(2)}, u32[]{:S(2)}) collective-permute-start(bf16[960,24]{0,1:T(8,128)(2,1)S(1)} %get-tuple-element.612), channel_id=1, source_target_pairs={{0,16},{8,24},{16,32},{24,40},{32,48},{40,56},{48,64},{56,72},{64,... | collective-permute-start | bytes 138248
  645.2 14.4 %collective-permute-start.4 = (bf16[960,24]{0,1:T(8,128)(2,1)S(1)}, bf16[960,24]{0,1:T(8,128)(2,1)S(1)}, u32[]{:S(2)}, u32[]{:S(2)}) collective-permute-start(bf16[960,24]{0,1:T(8,128)(2,1)S(1)} %get-tuple-element.612), channel_id=1, source_target_pairs={{0,8},{8,16},{16,24},{24,32},{32,40},{40,48},{48,56},{56,64},{64,7... | collective-permute-start | bytes 138248
  648.7 9.3 collective-permute-start.6
  651.1 9.8 collective-permute-start.7
  653.6 7.6 collective-permute-start
  658.0 5.8 collective-permute-start.8
  660.8 189.8 %all-reduce.23.cloned.1.call-start = ((), (), s32[]{:S(2)}) async-start(), calls=%async_computation.22 | async-start | bytes 524288
  663.8 259.3 %reduce-scatter.44.cloned.1.call-start = ((), (), s32[]{:S(2)}) async-start(), calls=%async_computation.20 | async-start | bytes 737280
  668.1 6.3 copy-start.42
  668.1 7.5 copy-start.2
  672.2 321.3 %reduce-scatter.42.cloned.1.call-start = ((), (), s32[]{:S(2)}) async-start(), calls=%async_computation.19 | async-start | bytes 552960
  679.3 8.6 copy-start.19
  684.1 3.8 copy-start.29
  684.1 4.2 copy-start.5
  684.1 4.2 copy-start.26
  686.3 377.6 %reduce-scatter.40.cloned.1.call-start = ((), (), s32[]{:S(2)}) async-start(), calls=%async_computation.18 | async-start | bytes 552960
  688.4 71.7 %copy-start.8 = (f32[128,960]{0,1:T(8,128)S(1)}, f32[128,960]{0,1:T(8,128)}, u32[]{:S(2)}) copy-start(f32[128,960]{0,1:T(8,128)} %copy-done.6) | copy-start | bytes 1474564
  (8 other events, 8.9 us)
Sparse Core Ops, SparseCore 0:
  68.2 33.8 all-gather.19
  122.8 34.4 all-gather.21
  159.6 33.8 all-gather.29
  195.7 34.3 all-gather.27
  231.6 40.1 all-gather.31
  273.4 39.7 all-gather.25
  314.8 39.4 all-gather.23
  388.2 79.7 reduce-scatter.35
  470.5 60.8 reduce-scatter.37
  533.6 76.3 reduce-scatter.33
  612.4 69.3 reduce-scatter.31
  684.9 80.3 all-reduce.20
  767.9 82.5 all-reduce.22
  854.0 69.0 reduce-scatter.43
  926.9 66.5 reduce-scatter.41
  997.3 66.5 reduce-scatter.39
where the time goes:
time: 1080 us; the launch traced here: 1070 us
  blocking collectives  450 us (42%)
  waiting for transfers between devices  431 us (40%)
  local copies, waits for them, and re-layouts  71.3 us (7%)
  matrix products  60.4 us (6%)
  starting transfers between devices  23.4 us (2%)
  between operations  16.8 us (2%)
  other arithmetic  13.4 us (1%)
    unnamed x32, waiting for transfers between devices  420 us
    unnamed x1, blocking collectives  97.2 us
    psum x1, blocking collectives, per_device(): gain_totals = lax.psum((attn_gain_term, ffn_gain_term), ('ctx', 'fsdp'))  68.6 us
    unnamed x126, local copies, waits for them, and re-layouts  48.6 us
    all_gather x1, blocking collectives, gather_weights(): lax.all_gather(key_weight, 'fsdp', axis=0, tiled=True)  36.1 us
    all_gather x1, blocking collectives, gather_weights(): lax.all_gather(up_weight, 'fsdp', axis=0, tiled=True)  35.5 us
    all_gather x1, blocking collectives, gather_weights(): lax.all_gather(gate_weight, 'fsdp', axis=0, tiled=True)  35 us
    all_gather x1, blocking collectives, gather_weights(): lax.all_gather(down_weight, 'fsdp', axis=0, tiled=True)  34.9 us
  transfers between devices with their start and end apart: 25, of which 8 were waited for; matrix products, arithmetic and copies ran while one was open for 19% of the time, Pallas kernels for 0%

commit v1 on v0

v1 whole, which is shorter than its diff:
```python
import functools

import jax
import jax.numpy as jnp
from jax import lax
from jax.experimental import pallas as pl
from jax.experimental.pallas import tpu as pltpu
from jax.sharding import PartitionSpec as P

D = 960
HEADS = 15
KVH = 5
HD = 64
NDOC = 4
QW = 960
KVW = 320
WIDE = 1024
TOK = 128

epsilon = 1e-05
block_rows = 512
masked_score = -1e30

MESH = pl.DeviceIdType.MESH
ANY = pl.BlockSpec(memory_space=pl.ANY)
VMEM = pl.BlockSpec(memory_space=pltpu.VMEM)
MIB = 1024 * 1024

ATTN_PARTS = ((0, 64), (64, 64), (128, 48))
ATTN_ROWS = 176
FFN_PARTS = ((0, 160), (160, 160), (320, 160))
FFN_ROWS = 480
HALF_FF = 1280
ORDERS = ((0, 1, 2), (1, 2, 0), (2, 0, 1))


def place():
    c = lax.axis_index("ctx")
    f = lax.axis_index("fsdp")
    x = lax.rem(lax.div(c, 2), 4)
    y = lax.div(f, 4) * 2 + lax.div(c, 8)
    return (x, y, lax.rem(f, 4)), lax.rem(c, 2)


def device(spot, core):
    x, y, z = spot
    return ((lax.rem(y, 2) * 4 + x) * 2 + core, lax.div(y, 2) * 4 + z)


def ring(value, by):
    return lax.rem(value + by + 4, 4)


def shifted(spot, axis, by):
    return tuple(ring(v, by) if i == axis else v for i, v in enumerate(spot))


def greet(devices):
    barrier = pltpu.get_barrier_semaphore()
    for target in devices:
        pl.semaphore_signal(barrier, inc=1, device_id=target, device_id_type=MESH)
    pl.semaphore_wait(barrier, len(devices))


def remote(src, dst, send, recv, target):
    copy = pltpu.make_async_remote_copy(
        src_ref=src, dst_ref=dst, send_sem=send, recv_sem=recv, device_id=target, device_id_type=MESH
    )
    copy.start()
    return copy


def view(ref, lead, spot, done, axis, position, rows, half=None):
    index = []
    cut = min(done) if (half is not None and done) else None
    for a in range(3):
        if a == cut:
            index.append(pl.ds(2 * half, 2))
        elif a in done:
            index.append(pl.ds(0, 4))
        elif a == axis:
            index.append(position)
        else:
            index.append(spot[a])
    low, count = rows
    if half is not None and not done:
        first = (count // 32) * 16
        low, count = (low, first) if half == 0 else (low + first, count - first)
    return ref.at[tuple(lead) + tuple(index) + (pl.ds(low, count),)]


def gather_kernel(
    attn_block, ffn_block, down_away, attn_all, ffn_all,
    ffn_own, down_in, send, recv, own_sem, pair_send, pair_recv,
):
    spot, core = place()
    sibling = device(spot, 1 - core)
    greet([device(shifted(spot, a, by), core) for a in range(3) for by in (1, -1)] + [sibling])
    down_copy = remote(down_away, down_in, pair_send.at[3], pair_recv.at[3], sibling)
    own_attn = pltpu.make_async_copy(attn_block, attn_all.at[core, spot[0], spot[1], spot[2]], own_sem.at[0])
    own_attn.start()
    ffn_own[...] = ffn_block[...]
    waiting, sent = {}, []

    def step(kind, stage, second):
        for part in (0, 1, 2):
            axis, done = ORDERS[part][stage], ORDERS[part][:stage]
            if kind == 0:
                whole, lead, rows, block = attn_all, (core,), ATTN_PARTS[part], attn_block
            else:
                whole, lead, rows, block = ffn_all, (), FFN_PARTS[part], ffn_own
            for copy in waiting.pop((kind, part), ()):
                copy.wait_recv()
            me = spot[axis]
            copies = []
            for way, by in enumerate((1, -1)):
                target = device(shifted(spot, axis, by), core)
                if second:
                    source = goal = view(whole, lead, spot, done, axis, ring(me, -by), rows, half=way)
                else:
                    source = goal = view(whole, lead, spot, done, axis, me, rows)
                    if stage == 0:
                        source = block.at[pl.ds(rows[0], rows[1])]
                copies.append(
                    remote(
                        source, goal,
                        send.at[kind, part, stage, second, way], recv.at[kind, part, stage, second, way], target,
                    )
                )
            waiting[kind, part] = copies
            sent.extend(copies)

    step(0, 0, 0)
    down_copy.wait_recv()
    ffn_own[pl.ds(320, 160)] = ffn_own[pl.ds(320, 160)] + down_in[...]
    own_ffn = pltpu.make_async_copy(ffn_own, ffn_all.at[spot[0], spot[1], spot[2]], own_sem.at[1])
    own_ffn.start()
    step(0, 0, 1)
    step(1, 0, 0)
    own_attn.wait()
    step(0, 1, 0)
    step(1, 0, 1)
    step(0, 1, 1)
    own_ffn.wait()
    step(1, 1, 0)
    step(0, 2, 0)
    step(1, 1, 1)
    step(0, 2, 1)
    step(1, 2, 0)
    pairs = []
    for part, rows in enumerate(ATTN_PARTS):
        for copy in waiting.pop((0, part)):
            copy.wait_recv()
        mine = attn_all.at[core, :, :, :, pl.ds(rows[0], rows[1])]
        pairs.append(remote(mine, mine, pair_send.at[part], pair_recv.at[part], sibling))
    step(1, 2, 1)
    for part in (0, 1, 2):
        for copy in waiting.pop((1, part)):
            copy.wait_recv()
    for copy in pairs:
        copy.wait()
    down_copy.wait_send()
    for copy in sent:
        copy.wait_send()


def gather_weights(attn_block, ffn_block, down_away):
    low = jnp.bfloat16
    return pl.pallas_call(
        gather_kernel,
        out_shape=(
            jax.ShapeDtypeStruct((2, 4, 4, 4, ATTN_ROWS, 128), low),
            jax.ShapeDtypeStruct((4, 4, 4, FFN_ROWS, 128), low),
        ),
        in_specs=[VMEM, VMEM, VMEM],
        out_specs=(ANY, ANY),
        scratch_shapes=[
            pltpu.VMEM((FFN_ROWS, 128), low),
            pltpu.VMEM((160, 128), low),
            pltpu.SemaphoreType.DMA((2, 3, 3, 2, 2)),
            pltpu.SemaphoreType.DMA((2, 3, 3, 2, 2)),
            pltpu.SemaphoreType.DMA((2,)),
            pltpu.SemaphoreType.DMA((4,)),
            pltpu.SemaphoreType.DMA((4,)),
        ],
        compiler_params=pltpu.CompilerParams(collective_id=1, has_side_effects=True, vmem_limit_bytes=16 * MIB),
        name="gather_weights",
    )(attn_block, ffn_block, down_away)


def add_into(target, terms):
    lead = target.shape[:-2]
    if not lead:
        total = target[...].astype(jnp.float32)
        for term in terms:
            total += term[...].astype(jnp.float32)
        target[...] = total.astype(target.dtype)
        return
    inner = lead[1] if len(lead) == 2 else 1

    def body(i, carry):
        at = (lax.div(i, inner), lax.rem(i, inner)) if len(lead) == 2 else (i,)
        total = target[at].astype(jnp.float32)
        for term in terms:
            total += term[at].astype(jnp.float32)
        target[at] = total.astype(target.dtype)
        return carry

    lax.fori_loop(0, lead[0] * inner, body, 0)


def reduce_shapes(rows):
    count = rows[1]
    first = (count // 32) * 16
    return (
        ((2, 4, count), (4, 4, count)),
        ((2, count), (4, count)),
        ((count - first,), (count,)),
    )


def reduce_kernel(attn_terms, ffn_terms, gain_terms, attn_out, ffn_out, down_out, gain_out, *scratch):
    attn, ffn, pair_in, gain_slots = scratch[:4]
    slots = scratch[4 : 4 + 36]
    load_sem, send, recv, pair_send, pair_recv, gain_send, gain_recv = scratch[40:]
    spot, core = place()
    sibling = device(spot, 1 - core)
    load_ffn = pltpu.make_async_copy(ffn_terms, ffn, load_sem.at[0])
    load_ffn.start()
    load_attn = pltpu.make_async_copy(attn_terms.at[core], attn, load_sem.at[1])
    load_attn.start()
    greet(
        [device(shifted(spot, a, by), core) for a in range(3) for by in (1, 2, 3)] + [sibling]
    )
    pair = remote(attn_terms.at[1 - core], pair_in, pair_send.at[0], pair_recv.at[0], sibling)
    waiting, sent = {}, [pair]

    def slot(kind, part, stage, second, way):
        ref = slots[((kind * 3 + part) * 3 + stage) * 2 + second]
        count = (ATTN_PARTS if kind == 0 else FFN_PARTS)[part][1]
        if stage == 2 and second == 0:
            first = (count // 32) * 16
            return ref.at[way, pl.ds(0, first if way == 0 else count - first)]
        return ref.at[way]

    def step(kind, stage, second):
        whole, parts = (attn, ATTN_PARTS) if kind == 0 else (ffn, FFN_PARTS)
        for part in (0, 1, 2):
            rows = parts[part]
            if stage < 3:
                axis, done = ORDERS[part][2 - stage], ORDERS[part][: 2 - stage]
            arrived = waiting.pop((kind, part), ())
            for copy in arrived:
                copy.wait_recv()
            if arrived and not second:
                before, full = ORDERS[part][3 - stage], ORDERS[part][: 3 - stage]
                add_into(
                    view(whole, (), spot, full, before, spot[before], rows),
                    [slot(kind, part, stage - 1, 1, way) for way in (0, 1)],
                )
            if stage == 3:
                goal = attn_out if kind == 0 else ffn_out
                goal[pl.ds(rows[0], rows[1])] = whole[spot[0], spot[1], spot[2], pl.ds(rows[0], rows[1])].astype(jnp.float32)
                continue
            me = spot[axis]
            copies = []
            for way, by in enumerate((1, -1)):
                target = device(shifted(spot, axis, by), core)
                if second:
                    add_into(
                        view(whole, (), spot, done, axis, ring(me, by), rows, half=way),
                        [slot(kind, part, stage, 0, way)],
                    )
                    source = view(whole, (), spot, done, axis, ring(me, by), rows)
                else:
                    source = view(whole, (), spot, done, axis, ring(me, 2), rows, half=way)
                copies.append(
                    remote(
                        source, slot(kind, part, stage, second, way),
                        send.at[kind, part, stage, second, way], recv.at[kind, part, stage, second, way], target,
                    )
                )
            waiting[kind, part] = copies
            sent.extend(copies)

    def gain_start(axis):
        me = spot[axis]
        gain_slots[axis, me] = gain_out[...]
        mine = gain_slots.at[axis, me]
        return [
            remote(mine, mine, gain_send.at[axis, by - 1], gain_recv.at[axis, by - 1], device(shifted(spot, axis, by), core))
            for by in (1, 2, 3)
        ]

    def gain_end(axis, copies):
        for copy in copies:
            copy.wait_recv()
        sent.extend(copies)
        gain_out[...] = (gain_slots[axis, 0] + gain_slots[axis, 1]) + (gain_slots[axis, 2] + gain_slots[axis, 3])

    gain_out[...] = gain_terms[...]
    load_ffn.wait()
    step(1, 0, 0)
    gains = gain_start(0)
    load_attn.wait()
    step(1, 0, 1)
    pair.wait_recv()
    for part in (0, 1, 2):
        rows = ATTN_PARTS[part]

        def add_pair(i, carry):
            at = (lax.div(i, 16), lax.rem(lax.div(i, 4), 4), lax.rem(i, 4), pl.ds(rows[0], rows[1]))
            attn[at] = (attn[at].astype(jnp.float32) + pair_in[at].astype(jnp.float32)).astype(attn.dtype)
            return carry

        lax.fori_loop(0, 64, add_pair, 0)
    step(0, 0, 0)
    gain_end(0, gains)
    gains = gain_start(1)
    step(1, 1, 0)
    step(0, 0, 1)
    step(1, 1, 1)
    gain_end(1, gains)
    gains = gain_start(2)
    step(0, 1, 0)
    step(1, 2, 0)
    step(0, 1, 1)
    step(1, 2, 1)
    gain_end(2, gains)
    gain_slots[3, core] = gain_out[...]
    mine = gain_slots.at[3, core]
    last = remote(mine, mine, pair_send.at[1], pair_recv.at[1], sibling)
    step(0, 2, 0)
    step(1, 3, 0)
    down_copy = remote(ffn_out.at[pl.ds(320, 160)], down_out, pair_send.at[2], pair_recv.at[2], sibling)
    step(0, 2, 1)
    last.wait_recv()
    gain_out[...] = gain_slots[3, 0] + gain_slots[3, 1]
    step(0, 3, 0)
    down_copy.wait_recv()
    sent.extend([last, down_copy])
    for copy in sent:
        copy.wait_send()


def reduce_grads(attn_terms, ffn_terms, gain_terms):
    low = jnp.bfloat16
    slots = []
    for parts in (ATTN_PARTS, FFN_PARTS):
        for rows in parts:
            for stage in reduce_shapes(rows):
                for shape in stage:
                    slots.append(pltpu.VMEM((2,) + shape + (128,), low))
    return pl.pallas_call(
        reduce_kernel,
        out_shape=(
            jax.ShapeDtypeStruct((ATTN_ROWS, 128), jnp.float32),
            jax.ShapeDtypeStruct((FFN_ROWS, 128), jnp.float32),
            jax.ShapeDtypeStruct((160, 128), jnp.float32),
            jax.ShapeDtypeStruct((16, 128), jnp.float32),
        ),
        in_specs=[ANY, ANY, VMEM],
        out_specs=(VMEM,) * 4,
        scratch_shapes=[
            pltpu.VMEM((4, 4, 4, ATTN_ROWS, 128), low),
            pltpu.VMEM((4, 4, 4, FFN_ROWS, 128), low),
            pltpu.VMEM((4, 4, 4, ATTN_ROWS, 128), low),
            pltpu.VMEM((4, 4, 16, 128), jnp.float32),
        ]
        + slots
        + [
            pltpu.SemaphoreType.DMA((2,)),
            pltpu.SemaphoreType.DMA((2, 3, 3, 2, 2)),
            pltpu.SemaphoreType.DMA((2, 3, 3, 2, 2)),
            pltpu.SemaphoreType.DMA((3,)),
            pltpu.SemaphoreType.DMA((3,)),
            pltpu.SemaphoreType.DMA((3, 3)),
            pltpu.SemaphoreType.DMA((3, 3)),
        ],
        compiler_params=pltpu.CompilerParams(collective_id=2, has_side_effects=True, vmem_limit_bytes=48 * MIB),
        name="reduce_grads",
    )(attn_terms, ffn_terms, gain_terms)


def keys_kernel(block, out, own_sem, send, recv, pair_send, pair_recv):
    spot, core = place()
    x, y, z = spot
    half = lax.rem(y, 2)
    sibling = device(spot, 1 - core)
    across = device((x, y + 1 - 2 * half, z), core)
    greet([device(shifted(spot, 0, by), core) for by in (1, -1)] + [across, sibling])
    mine = out.at[half, x, core]
    own = pltpu.make_async_copy(block, mine, own_sem)
    own.start()
    sent, pairs = [], []

    def pass_on(ref):
        pairs.append(remote(ref, ref, pair_send.at[len(pairs)], pair_recv.at[len(pairs)], sibling))

    over = remote(block, mine, send.at[0], recv.at[0], across)
    pairs.append(remote(block, mine, pair_send.at[0], pair_recv.at[0], sibling))
    first = [
        remote(block, mine, send.at[1 + way], recv.at[1 + way], device(shifted(spot, 0, by), core))
        for way, by in enumerate((1, -1))
    ]
    over.wait_recv()
    other = out.at[1 - half, x, core]
    second = [
        remote(other, other, send.at[3 + way], recv.at[3 + way], device(shifted(spot, 0, by), core))
        for way, by in enumerate((1, -1))
    ]
    pass_on(other)
    last = []
    for way, by in enumerate((1, -1)):
        first[way].wait_recv()
        if way == 0:
            ref = out.at[half, ring(x, -by), core]
            last.append(remote(ref, ref, send.at[5], recv.at[5], device(shifted(spot, 0, by), core)))
        pass_on(out.at[half, ring(x, -by), core])
    for way, by in enumerate((1, -1)):
        second[way].wait_recv()
        if way == 1:
            ref = out.at[1 - half, ring(x, -by), core]
            last.append(remote(ref, ref, send.at[6], recv.at[6], device(shifted(spot, 0, by), core)))
        pass_on(out.at[1 - half, ring(x, -by), core])
    last[0].wait_recv()
    pass_on(out.at[half, ring(x, 2), core])
    last[1].wait_recv()
    pass_on(out.at[1 - half, ring(x, 2), core])
    own.wait()
    for copy in pairs:
        copy.wait()
    for copy in [over] + first + second + last:
        copy.wait_send()


def gather_keys(block):
    return pl.pallas_call(
        keys_kernel,
        out_shape=jax.ShapeDtypeStruct((2, 4, 2, TOK, 2 * KVW), jnp.bfloat16),
        in_specs=[VMEM],
        out_specs=ANY,
        scratch_shapes=[
            pltpu.SemaphoreType.DMA,
            pltpu.SemaphoreType.DMA((7,)),
            pltpu.SemaphoreType.DMA((7,)),
            pltpu.SemaphoreType.DMA((8,)),
            pltpu.SemaphoreType.DMA((8,)),
        ],
        compiler_params=pltpu.CompilerParams(collective_id=3, has_side_effects=True),
        name="gather_keys",
    )(block)


def key_grads_kernel(terms, total, mine, pair_in, far_in, near_in, across_in, send, recv, load_sem):
    spot, core = place()
    x, y, z = spot
    half = lax.rem(y, 2)
    sibling = device(spot, 1 - core)
    across = device((x, y + 1 - 2 * half, z), core)
    loads = []
    for h in (0, 1):
        for i in range(4):
            load = pltpu.make_async_copy(terms.at[h, i, core], mine.at[h, i], load_sem.at[h, i])
            load.start()
            loads.append(load)
    greet([device(shifted(spot, 0, by), core) for by in (1, -1)] + [across, sibling])
    pairs = []
    for k, by in enumerate((2, 1, 3, 0)):
        for h in (0, 1):
            at = ring(x, by)
            pairs.append(
                remote(terms.at[h, at, 1 - core], pair_in.at[h, at], send.at[2 * k + h], recv.at[2 * k + h], sibling)
            )
    for load in loads:
        load.wait()

    def add(goal, *sources):
        sum_ = goal[...].astype(jnp.float32)
        for source in sources:
            sum_ += source[...].astype(jnp.float32)
        goal[...] = sum_.astype(goal.dtype)

    for h in (0, 1):
        pairs[h].wait_recv()
        add(mine.at[h, ring(x, 2)], pair_in.at[h, ring(x, 2)])
    far = [
        remote(mine.at[way, ring(x, 2)], far_in.at[way], send.at[8 + way], recv.at[8 + way], device(shifted(spot, 0, by), core))
        for way, by in enumerate((1, -1))
    ]
    for pair in pairs[2:]:
        pair.wait_recv()
    for by in (1, 3, 0):
        for h in (0, 1):
            add(mine.at[h, ring(x, by)], pair_in.at[h, ring(x, by)])
    near = []
    for way, by in enumerate((1, -1)):
        far[way].wait_recv()
        add(mine.at[way, ring(x, by)], far_in.at[way])
        near.append(
            remote(
                mine.at[:, ring(x, by)], near_in.at[way], send.at[10 + way], recv.at[10 + way],
                device(shifted(spot, 0, by), core),
            )
        )
    for copy in near:
        copy.wait_recv()
    add(mine.at[1 - half, x], near_in.at[0, 1 - half], near_in.at[1, 1 - half])
    last = remote(mine.at[1 - half, x], across_in, send.at[12], recv.at[12], across)
    add(mine.at[half, x], near_in.at[0, half], near_in.at[1, half])
    last.wait_recv()
    total[...] = mine[half, x].astype(jnp.float32) + across_in[...].astype(jnp.float32)
    for copy in pairs + far + near + [last]:
        copy.wait_send()


def reduce_keys(terms):
    low = jnp.bfloat16
    wide = 2 * KVW
    return pl.pallas_call(
        key_grads_kernel,
        out_shape=jax.ShapeDtypeStruct((TOK, wide), jnp.float32),
        in_specs=[ANY],
        out_specs=VMEM,
        scratch_shapes=[
            pltpu.VMEM((2, 4, TOK, wide), low),
            pltpu.VMEM((2, 4, TOK, wide), low),
            pltpu.VMEM((2, TOK, wide), low),
            pltpu.VMEM((2, 2, TOK, wide), low),
            pltpu.VMEM((TOK, wide), low),
            pltpu.SemaphoreType.DMA((13,)),
            pltpu.SemaphoreType.DMA((13,)),
            pltpu.SemaphoreType.DMA((2, 4)),
        ],
        compiler_params=pltpu.CompilerParams(collective_id=4, has_side_effects=True, vmem_limit_bytes=24 * MIB),
        name="reduce_keys",
    )(terms)


def dot(left, right, left_dim=1, right_dim=0):
    return lax.dot_general(left, right, (((left_dim,), (right_dim,)), ((), ())), preferred_element_type=jnp.float32)


def ffn_kernel(
    residual, gain, cot, weights,
    layer_out, d_residual, gain_term, grads,
    gate_w, up_w, down_w, tokens, cots, out_sum, norm_sum, out_in, norm_in, load_sem, send, recv,
):
    spot, core = place()
    sibling = device(spot, 1 - core)
    for part, goal in enumerate((gate_w, up_w, down_w)):

        def load(i, carry):
            x, y, z = lax.div(i, 16), lax.rem(lax.div(i, 4), 4), lax.rem(i, 4)
            rows = lax.rem(y, 2) * 4 + x
            lanes = lax.div(y, 2) * 4 + z
            if part == 2:
                rows, lanes = lanes, rows
            pltpu.make_async_copy(
                weights.at[x, y, z, pl.ds(160 * part, 160)],
                goal.at[pl.ds(pl.multiple_of(rows * 160, 32), 160), pl.ds(pl.multiple_of(lanes * 128, 128), 128)],
                load_sem.at[part],
            ).start()
            return carry

        lax.fori_loop(0, 64, load, 0)
    greet([sibling])
    cots[pl.ds(0, TOK)] = cot[...]
    cot_copy = remote(cot, cots.at[pl.ds(TOK, TOK)], send.at[0], recv.at[0], sibling)
    res = residual[...]
    scale = lax.rsqrt(jnp.sum(res * res, axis=-1, keepdims=True) * (1.0 / D) + epsilon)
    tokens[pl.ds(0, TOK)] = (res * scale * gain[...]).astype(jnp.bfloat16)
    token_copy = remote(tokens.at[pl.ds(0, TOK)], tokens.at[pl.ds(TOK, TOK)], send.at[1], recv.at[1], sibling)
    out_sum[...] = jnp.zeros_like(out_sum)
    norm_sum[...] = jnp.zeros_like(norm_sum)
    cot_copy.wait_recv()
    token_copy.wait_recv()
    for part, goal in enumerate((gate_w, up_w, down_w)):
        pltpu.make_async_copy(goal, goal, load_sem.at[part]).wait()

    def chunk(j, carry):
        rows = pl.ds(pl.multiple_of(j * 320, 320), 320)
        gate_rows, up_rows, down_rows = gate_w[rows, :], up_w[rows, :], down_w[rows, :]
        both, cot_both = tokens[...], cots[...]
        gate_value = dot(both, gate_rows, 1, 1)
        up_value = dot(both, up_rows, 1, 1)
        d_hidden = dot(cot_both, down_rows, 1, 1)
        sigmoid = 1.0 / (1.0 + jnp.exp(-gate_value))
        silu = gate_value * sigmoid
        hidden = (silu * up_value).astype(jnp.bfloat16)
        d_gate = (d_hidden * up_value * sigmoid * (1.0 + gate_value * (1.0 - sigmoid))).astype(jnp.bfloat16)
        d_up = (d_hidden * silu).astype(jnp.bfloat16)
        out_sum[...] += dot(hidden, down_rows)
        norm_sum[...] += dot(d_gate, gate_rows) + dot(d_up, up_rows)
        for part, (left, right) in enumerate(((d_gate, both), (d_up, both), (hidden, cot_both))):
            term = dot(left, right, 0, 0).astype(jnp.bfloat16)
            for u in range(2):
                for lane in range(8):
                    piece = term[160 * u : 160 * u + 160, 128 * lane : 128 * lane + 128]
                    block = 2 * j + u
                    if part == 2:
                        at = (lane % 4, lax.div(block, 4) * 2 + lane // 4, lax.rem(block, 4))
                    else:
                        at = (lax.rem(block, 4), (lane // 4) * 2 + lax.div(block, 4), lane % 4)
                    grads[at + (pl.ds(160 * part, 160),)] = piece
        return carry

    lax.fori_loop(0, 4, chunk, 0)
    theirs = pl.ds(TOK, TOK)
    norm_copy = remote(norm_sum.at[theirs], norm_in, send.at[2], recv.at[2], sibling)
    out_copy = remote(out_sum.at[theirs], out_in, send.at[3], recv.at[3], sibling)
    norm_copy.wait_recv()
    d_normed = norm_sum[pl.ds(0, TOK)] + norm_in[...]
    gain_term[...] = jnp.sum(d_normed * res * scale, axis=0, keepdims=True)
    u = d_normed * gain[...]
    d_residual[...] = cot[...].astype(jnp.float32) + scale * (
        u - res * scale * scale * (jnp.sum(u * res, axis=-1, keepdims=True) * (1.0 / D))
    )
    out_copy.wait_recv()
    layer_out[...] = (res + out_sum[pl.ds(0, TOK)] + out_in[...]).astype(jnp.bfloat16)
    for copy in (cot_copy, token_copy, norm_copy, out_copy):
        copy.wait_send()


def ffn(residual, gain, cot, weights):
    low = jnp.bfloat16
    return pl.pallas_call(
        ffn_kernel,
        out_shape=(
            jax.ShapeDtypeStruct((TOK, WIDE), low),
            jax.ShapeDtypeStruct((TOK, WIDE), jnp.float32),
            jax.ShapeDtypeStruct((1, WIDE), jnp.float32),
            jax.ShapeDtypeStruct((4, 4, 4, FFN_ROWS, 128), low),
        ),
        in_specs=[VMEM, VMEM, VMEM, ANY],
        out_specs=(VMEM,) * 4,
        scratch_shapes=[pltpu.VMEM((HALF_FF, WIDE), low)] * 3
        + [pltpu.VMEM((2 * TOK, WIDE), low)] * 2
        + [pltpu.VMEM((2 * TOK, WIDE), jnp.float32)] * 2
        + [pltpu.VMEM((TOK, WIDE), jnp.float32)] * 2
        + [
            pltpu.SemaphoreType.DMA((3,)),
            pltpu.SemaphoreType.DMA((4,)),
            pltpu.SemaphoreType.DMA((4,)),
        ],
        compiler_params=pltpu.CompilerParams(collective_id=5, has_side_effects=True, vmem_limit_bytes=48 * MIB),
        name="ffn",
    )(residual, gain, cot, weights)


def spread(array, axis):
    shape = array.shape
    split = array.reshape(shape[:axis] + (shape[axis] // 60, 60) + shape[axis + 1 :])
    pads = [(0, 0)] * split.ndim
    pads[axis + 1] = (0, 4)
    return jnp.pad(split, pads).reshape(shape[:axis] + (shape[axis] // 60 * 64,) + shape[axis + 1 :])


def squeeze(array, axis):
    shape = array.shape
    split = array.reshape(shape[:axis] + (shape[axis] // 64, 64) + shape[axis + 1 :])
    split = lax.slice_in_dim(split, 0, 60, axis=axis + 1)
    return split.reshape(shape[:axis] + (shape[axis] // 64 * 60,) + shape[axis + 1 :])


def layout(offsets, token_index):
    inner = offsets[1:NDOC]
    after = token_index[:, None] >= inner[None, :]
    segment = jnp.sum(after.astype(jnp.int32), axis=1)
    starts = jnp.max(jnp.where(after, inner[None, :], 0), axis=1)
    return (segment, token_index - starts)


def rotary(positions):
    half_dim = HD // 2
    rate_table = 10000.0 ** (-2.0 * jnp.arange(half_dim, dtype=jnp.float32) / HD)
    angles = positions.astype(jnp.float32)[:, None] * rate_table[None, :]
    cosine = jnp.cos(angles)
    sine_table = jnp.sin(angles)
    return (
        jnp.concatenate([cosine, cosine], axis=1),
        jnp.concatenate([sine_table, sine_table], axis=1),
    )


def turn_half(vectors):
    half_dim = HD // 2
    return jnp.concatenate([-vectors[..., half_dim:], vectors[..., :half_dim]], axis=-1)


def rotate(vectors, cosine, sine_table):
    return vectors * cosine[:, None, :] + turn_half(vectors) * sine_table[:, None, :]


def unrotate(vectors, cosine, sine_table):
    return vectors * cosine[:, None, :] - turn_half(vectors) * sine_table[:, None, :]


def pack_weights(query, key, value, proj, gate, up, down, core):
    columns = lambda a: spread(a.T, 1)
    zeros = jnp.zeros((4, 128), jnp.bfloat16)
    attn = jnp.concatenate(
        [columns(query), zeros, columns(proj), zeros, columns(key), columns(value), zeros, zeros], axis=0
    )
    left = jnp.pad(down, ((0, 0), (0, 68)))
    right = jnp.pad(down, ((0, 0), (64, 4)))
    placed = jnp.where(core == 0, left, right)
    keep = jnp.where(core == 0, placed[:160], placed[160:])
    away = jnp.where(core == 0, placed[160:], placed[:160])
    return attn, jnp.concatenate([columns(gate), columns(up), keep], axis=0), away


def per_device(
    inputs, doc_offsets, attn_gain, query_weight, key_weight, value_weight, proj_weight,
    ffn_gain, gate_weight, up_weight, down_weight, cotangent,
):
    low = jnp.bfloat16
    row_count = TOK
    length = row_count * 16
    group_size = HEADS // KVH
    score_scale = HD ** (-0.5)
    _, core = place()
    first_row = lax.axis_index("ctx") * row_count
    last_row = first_row + row_count - 1
    offsets = doc_offsets[0]
    token_index = first_row + jnp.arange(row_count, dtype=jnp.int32)
    segment, positions = layout(offsets, token_index)
    cosine, sine_table = rotary(positions)
    attn_all, ffn_all = gather_weights(
        *pack_weights(query_weight, key_weight, value_weight, proj_weight, gate_weight, up_weight, down_weight, core)
    )
    attn_wide = jnp.transpose(
        attn_all.reshape(2, 4, 2, 2, 4, ATTN_ROWS, 128), (3, 1, 0, 5, 2, 4, 6)
    ).reshape(16, ATTN_ROWS, WIDE)
    query_w = attn_wide[:, :64].reshape(WIDE, WIDE)
    proj_w = attn_wide[:, 64:128].reshape(WIDE, WIDE)
    key_value_w = attn_wide[:, 128:176].reshape(768, WIDE)

    tokens = spread(inputs[0], 1).astype(jnp.float32)
    gain_wide = spread(attn_gain[None], 1)
    ffn_gain_wide = spread(ffn_gain[None], 1)
    cot_low = spread(cotangent[0], 1)
    attn_scale = lax.rsqrt(jnp.sum(tokens * tokens, axis=-1, keepdims=True) * (1.0 / D) + epsilon)
    normed = (tokens * attn_scale * gain_wide).astype(low)
    queries = squeeze(dot(normed, query_w, 1, 1), 1)
    key_value = dot(normed, key_value_w, 1, 1).reshape(row_count, 16, 48)
    keys_flat = key_value[:, :, :20].reshape(row_count, KVW)
    value_rows = key_value[:, :, 20:40].reshape(row_count, KVW).astype(low)
    query_rot = (
        rotate(queries.reshape(row_count, HEADS, HD), cosine, sine_table)
        .astype(low)
        .reshape(row_count, KVH, group_size, HD)
    )
    key_rot = rotate(keys_flat.reshape(row_count, KVH, HD), cosine, sine_table).astype(low).reshape(row_count, KVW)
    gathered = gather_keys(jnp.concatenate([key_rot, value_rows], axis=1)).reshape(length, 2, KVH, HD)
    all_keys, all_values = gathered[:, 0], gathered[:, 1]

    def block_scores(key_block, key_start):
        key_index = key_start + jnp.arange(key_block.shape[0], dtype=jnp.int32)
        key_segment = layout(offsets, key_index)[0]
        allowed = (segment[:, None] == key_segment[None, :]) & (
            key_index[None, :] <= token_index[:, None]
        )
        scores = (
            jnp.einsum("qhgd,khd->hgqk", query_rot, key_block, preferred_element_type=jnp.float32)
            * score_scale
        )
        return jnp.where(allowed[None, None], scores, masked_score)

    def visit(carried, key_block, value_block, key_start):

        def update(current):
            row_top, row_total, weighted = current
            scores = block_scores(key_block, key_start)
            new_top = jnp.maximum(row_top, jnp.max(scores, axis=-1))
            factor = jnp.exp(row_top - new_top)
            raised = jnp.exp(scores - new_top[..., None])
            new_total = row_total * factor + jnp.sum(raised, axis=-1)
            added = jnp.einsum(
                "hgqk,khd->qhgd",
                raised.astype(low),
                value_block,
                preferred_element_type=jnp.float32,
            )
            return (
                new_top,
                new_total,
                weighted * jnp.transpose(factor, (2, 0, 1))[..., None] + added,
            )

        return lax.cond(key_start <= last_row, update, lambda current: current, carried)

    initial = (
        jnp.full((KVH, group_size, row_count), masked_score, jnp.float32),
        jnp.zeros((KVH, group_size, row_count), jnp.float32),
        jnp.zeros((row_count, KVH, group_size, HD), jnp.float32),
    )
    steps_count = length // block_rows

    def scan_step(current, element):
        return (visit(current, element[0], element[1], element[2] * block_rows), None)

    row_top, row_total, weighted = lax.scan(
        scan_step,
        initial,
        (
            all_keys.reshape(steps_count, block_rows, KVH, HD),
            all_values.reshape(steps_count, block_rows, KVH, HD),
            jnp.arange(steps_count, dtype=jnp.int32),
        ),
    )[0]
    log_total = row_top + jnp.log(row_total)
    mixed = weighted / jnp.transpose(row_total, (2, 0, 1))[..., None]
    attn_out = spread(mixed.astype(low).reshape(row_count, QW), 1)
    residual = tokens + dot(attn_out, proj_w, 1, 1)

    layer_out, d_residual, ffn_gain_term, ffn_terms = ffn(residual, ffn_gain_wide, cot_low, ffn_all)

    d_branch = d_residual.astype(low)
    d_mixed = squeeze(dot(d_branch, proj_w).astype(low), 1).reshape(row_count, KVH, group_size, HD)
    row_delta = jnp.transpose(jnp.sum(d_mixed.astype(jnp.float32) * mixed, axis=-1), (1, 2, 0))
    empty_block = jnp.zeros((block_rows, KVW), jnp.float32)

    def backward_step(d_query, element):
        key_block, value_block, block_index = element
        key_start = block_index * block_rows

        def contribute(pending):
            shares = jnp.exp(block_scores(key_block, key_start) - log_total[..., None])
            d_shares = jnp.einsum(
                "qhgd,khd->hgqk", d_mixed, value_block, preferred_element_type=jnp.float32
            )
            d_scores = (shares * (d_shares - row_delta[..., None])).astype(low)
            d_query_add = (
                jnp.einsum(
                    "hgqk,khd->qhgd", d_scores, key_block, preferred_element_type=jnp.float32
                )
                * score_scale
            )
            d_key_block = (
                jnp.einsum(
                    "hgqk,qhgd->khd", d_scores, query_rot, preferred_element_type=jnp.float32
                )
                * score_scale
            )
            d_value_block = jnp.einsum(
                "hgqk,qhgd->khd",
                shares.astype(low),
                d_mixed,
                preferred_element_type=jnp.float32,
            )
            return (
                pending + d_query_add,
                d_key_block.reshape(block_rows, KVW),
                d_value_block.reshape(block_rows, KVW),
            )

        def skipped(pending):
            return (pending, empty_block, empty_block)

        d_query, d_key_block, d_value_block = lax.cond(
            key_start <= last_row, contribute, skipped, d_query
        )
        return (d_query, (d_key_block, d_value_block))

    d_query_rot, stacked = lax.scan(
        backward_step,
        jnp.zeros((row_count, KVH, group_size, HD), jnp.float32),
        (
            all_keys.reshape(steps_count, block_rows, KVH, HD),
            all_values.reshape(steps_count, block_rows, KVH, HD),
            jnp.arange(steps_count, dtype=jnp.int32),
        ),
    )
    sums = reduce_keys(
        jnp.concatenate([stacked[0].reshape(length, KVW), stacked[1].reshape(length, KVW)], axis=1)
        .astype(low)
        .reshape(2, 4, 2, row_count, 2 * KVW)
    )
    d_queries = spread(
        unrotate(d_query_rot.reshape(row_count, HEADS, HD), cosine, sine_table).astype(low).reshape(row_count, QW), 1
    )
    d_keys = unrotate(sums[:, :KVW].reshape(row_count, KVH, HD), cosine, sine_table).astype(low)
    d_values = sums[:, KVW:].astype(low)
    d_key_value = jnp.concatenate(
        [d_keys.reshape(row_count, 16, 20), d_values.reshape(row_count, 16, 20), jnp.zeros((row_count, 16, 8), low)],
        axis=2,
    ).reshape(row_count, 768)
    d_normed = dot(d_queries, query_w) + dot(d_key_value, key_value_w)
    attn_gain_term = jnp.sum(d_normed * tokens * attn_scale, axis=0, keepdims=True)
    scaled_attn = d_normed * gain_wide
    d_tokens = d_residual + attn_scale * (
        scaled_attn
        - tokens * attn_scale * attn_scale * (jnp.sum(scaled_attn * tokens, axis=-1, keepdims=True) * (1.0 / D))
    )
    attn_terms = jnp.concatenate(
        [
            dot(d_queries, normed, 0, 0).astype(low).reshape(16, 64, 8, 128),
            dot(d_branch, attn_out, 0, 0).astype(low).reshape(16, 64, 8, 128),
            dot(d_key_value, normed, 0, 0).astype(low).reshape(16, 48, 8, 128),
        ],
        axis=1,
    )
    attn_terms = jnp.transpose(attn_terms.reshape(2, 4, 2, ATTN_ROWS, 2, 4, 128), (2, 1, 4, 0, 5, 3, 6)).reshape(
        2, 4, 4, 4, ATTN_ROWS, 128
    )
    gain_terms = jnp.concatenate([attn_gain_term.reshape(8, 128), ffn_gain_term.reshape(8, 128)], axis=0)
    attn_sum, ffn_sum, down_other, gains = reduce_grads(attn_terms, ffn_terms, gain_terms)
    columns = lambda a: squeeze(a, 1).T
    down_mine = ffn_sum[320:]
    down_both = jnp.concatenate(
        [jnp.where(core == 0, down_mine, down_other), jnp.where(core == 0, down_other, down_mine)], axis=0
    )
    return (
        squeeze(layer_out, 1)[None],
        squeeze(d_tokens.astype(low), 1)[None],
        squeeze(gains[:8].reshape(WIDE), 0),
        columns(attn_sum[:60]),
        columns(attn_sum[128:148]),
        columns(attn_sum[148:168]),
        columns(attn_sum[64:124]),
        squeeze(gains[8:].reshape(WIDE), 0),
        columns(ffn_sum[:160]),
        columns(ffn_sum[160:320]),
        jnp.where(core == 0, down_both[:, :60], down_both[:, 64:124]),
    )


def solution(mesh):
    split = P("fsdp", "ctx")
    rows = P("fsdp", "ctx", None)
    return jax.shard_map(
        per_device,
        mesh=mesh,
        in_specs=(rows, P("fsdp", None), P(), split, split, split, split, P(), split, split, split, rows),
        out_specs=(rows, rows, P(), split, split, split, split, P(), split, split, split),
        check_vma=False,
    )
```

time: 1080 us -> 361 us (0.33)
  blocking collectives: 450 us -> 0 us
  waiting for transfers between devices: 431 us -> 0 us
  Pallas kernels: 0 us -> 212 us
  matrix products: 60.4 us -> 24.7 us
  local copies, waits for them, and re-layouts: 71.3 us -> 103 us
  starting transfers between devices: 23.4 us -> 0 us
  between operations: 16.8 us -> 1.63 us
    unnamed x32 -> x0, waiting for transfers between devices: 420 us -> none
    all_gather x9 -> x0, blocking collectives: 284 us -> none  [the longest x1 36.1 us: gather_weights(): lax.all_gather(key_weight, 'fsdp', axis=0, tiled=True)]
    pallas_call x0 -> x5, Pallas kernels: none -> 212 us  [the longest x1 59.2 us: reduce_keys(): pl.pallas_call(key_grads_kernel, out_shape=jax.ShapeDtypeStruct((TOK, wid...]
    unnamed x1 -> x0, blocking collectives: 97.2 us -> none
    psum x1 -> x0, blocking collectives: 68.6 us -> none  [per_device(): gain_totals = lax.psum((attn_gain_term, ffn_gain_term), ('ctx', 'fsdp'))]
    unnamed x126 -> x56, local copies, waits for them, and re-layouts: 48.6 us -> 10.7 us
    dot_general x23 -> x11, matrix products: 55.4 us -> 19.6 us  [the longest x9 15.5 us: dot(): lax.dot_general(left, right, (((left_dim,), (right_dim,)), ((), ())), pre...]
    unnamed x16 -> x0, starting transfers between devices: 23 us -> none
  transfers between devices with their start and end apart: 25 -> 0, of which waited for: 8 -> 0; matrix products, arithmetic and copies ran while one was open for 19% -> 0% of each run, Pallas kernels for 0% -> 0%
where the time goes in v1:
time: 361 us; the launch traced here: 359 us
  Pallas kernels  212 us (59%)
  local copies, waits for them, and re-layouts  103 us (29%)
  matrix products  24.7 us (7%)
  other arithmetic  12.1 us (3%)
  loops' own time  5.82 us (2%)
    pallas_call x1, Pallas kernels, reduce_keys(): pl.pallas_call(key_grads_kernel, out_shape=jax.ShapeDtypeStruct((TOK, wid...  59.2 us
    pallas_call x1, Pallas kernels, gather_weights(): pl.pallas_call(gather_kernel, out_shape=(jax.ShapeDtypeStruct((2, 4, 4, 4...  56 us
    pallas_call x1, Pallas kernels, reduce_grads(): pl.pallas_call(reduce_kernel, out_shape=(jax.ShapeDtypeStruct((ATTN_ROWS,...  55.6 us
    pallas_call x1, Pallas kernels, ffn(): pl.pallas_call(ffn_kernel, out_shape=(jax.ShapeDtypeStruct((TOK, WIDE), l...  20.7 us
    pallas_call x1, Pallas kernels, gather_keys(): pl.pallas_call(keys_kernel, out_shape=jax.ShapeDtypeStruct((2, 4, 2, TOK,...  19.9 us
    concatenate x6, local copies, waits for them, and re-layouts, per_device(): jnp.concatenate([dot(d_queries, normed, 0, 0).astype(low).reshape(16, 64,...  17.2 us
    dot_general x9, matrix products, dot(): lax.dot_general(left, right, (((left_dim,), (right_dim,)), ((), ())), pre...  15.5 us
    unnamed x56, local copies, waits for them, and re-layouts  10.7 us

profile of v1, /device:TPU:0, one launch (start us, length us, event | category | flops | bytes accessed | tf_op | source)
XLA Modules:
  0.0 359.0 jit_solution(12523918417529317032)
XLA Ops:
  0.7 0.9 copy.143
  1.7 0.9 copy.141
  2.7 0.9 copy.142
  3.8 0.8 reshape.430
  4.8 0.8 reshape.432
  5.7 0.8 reshape.434
  6.6 0.8 reshape.436
  7.7 56.0 %gather_weights.1 = (bf16[2,4,4,4,176,128]{5,4,3,2,1,0:T(8,128)(2,1)S(1)}, bf16[4,4,4,480,128]{4,3,2,1,0:T(8,128)(2,1)S(1)}) custom-call(bf16[176,128]{1,0:T(8,128)(2,1)S(1)} %concatenate.64.attn_block, bf16[480,128]{1,0:T(8,128)(2,1)S(1)} %pad_maximum_fusion.4.ffn_block, bf16[160,128]{1,0:T(8,128)(2,1)S(1)} %get-tuple-element.657.down_away), custom_call_target="tpu_custom_call" | custom-call | tf_op jit(solution)/shard_map/gather_weights/pallas_call | solution.py:169
  63.7 3.1 copy-done
  66.8 5.2 %copy.147 = bf16[2,4,2,176,2,4,128]{6,5,4,3,2,1,0:T(4,128)(2,1)} copy(bf16[2,4,2,176,2,4,128]{6,3,5,0,4,1,2:T(8,128)(2,1)S(1)} %bitcast.235) | data formatting | bytes 11534336 | tf_op jit(solution)/shard_map/transpose | solution.py:732
  72.0 10.4 %reshape.443 = bf16[16,176,1024]{2,1,0:T(8,128)(2,1)} reshape(bf16[2,4,2,176,2,4,128]{6,5,4,3,2,1,0:T(4,128)(2,1)} %copy.147) | data formatting | bytes 11534336 | tf_op jit(solution)/shard_map/reshape | solution.py:734
  83.0 2.4 fusion.51
  86.0 2.0 fusion.55
  88.6 0.8 pad_maximum_fusion.3.block
  89.4 19.9 %gather_keys.1 = bf16[2,4,2,128,640]{4,3,2,1,0:T(8,128)(2,1)} custom-call(bf16[128,640]{1,0:T(8,128)(2,1)} %pad_maximum_fusion.3.block), custom_call_target="tpu_custom_call" | custom-call | tf_op jit(solution)/shard_map/gather_keys/pallas_call | solution.py:438
  109.3 7.5 %copy.152 = bf16[2,4,2,128,640]{3,2,1,0,4:T(2,128)(2,1)} copy(bf16[2,4,2,128,640]{4,3,2,1,0:T(8,128)(2,1)} %gather_keys.1) | data formatting | bytes 5242880 | tf_op jit(solution)/shard_map/gather_keys/pallas_call | solution.py:438
  116.8 4.3 %reshape.444 = bf16[2048,2,5,64]{0,3,2,1:T(8,128)(2,1)S(1)} reshape(bf16[2,4,2,128,640]{3,2,1,0,4:T(2,128)(2,1)} %copy.152) | data formatting | bytes 5242880 | tf_op jit(solution)/shard_map/reshape | solution.py:755
  121.1 1.8 fusion.75
  122.9 4.1 %reshape_squeeze.15 = bf16[4,512,5,64]{1,0,3,2:T(4,128)(2,1)} reshape(bf16[2048,1,5,64]{0,3,2,1:T(8,128)(2,1)} %get-tuple-element.640) | data formatting | bytes 2621440 | tf_op jit(solution)/shard_map/reshape;squeeze | solution.py:807
  127.0 1.6 copy.154
  128.6 4.1 %reshape_squeeze.16 = bf16[4,512,5,64]{1,0,3,2:T(4,128)(2,1)} reshape(bf16[2048,1,5,64]{0,3,2,1:T(8,128)(2,1)} %get-tuple-element.639) | data formatting | bytes 2621440 | tf_op jit(solution)/shard_map/reshape;squeeze | solution.py:808
  132.7 2.7 copy.155
  135.5 9.5 %while.33 = (s32[]{:T(128)}, f32[5,3,128]{2,1,0:T(4,128)S(1)}, f32[5,3,128]{2,1,0:T(4,128)S(1)}, f32[128,5,3,64]{0,3,2,1:T(8,128)S(1)}, s32[4]{0:T(128)S(1)}, /*...) while((s32[]{:T(128)}, f32[5,3,128]{2,1,0:T(4,128)S(1)}, ...), condition=%wide.region_9.10_spmd.clone, body=%wide.region_3.9_spmd.clone.sunk | while | flops 262924544 | bytes 14079347 | solution.py:803
  136.9 4.1 %conditional.6 = ((f32[5,3,128]{2,1,0:T(4,128)S(1)}, f32[5,3,128]{2,1,0:T(4,128)S(1)}, f32[128,5,3,64]{0,3,2,1:T(8,128)S(1)})) conditional(s32[]{:T(128)} %convert_element_type.190, (f32[5,3,128]{2,1,0:T(4,128)S(1)}, f32[5,3,128]{2,1,0:T(4,128)S(1)}, f32[128,5,3,64]{0,3,2,1:T(8,128)S(1)}) %tuple.105, (s32[128]{0:T(128)S(1)}, s32[]{:T(128)}, ...), branch_computations={%region_4.4_spmd, %region_5.8_spmd} | conditional | flops 262924544 | bytes 14078544 | solution.py:791
  137.3 0.8 fusion.6
  138.1 2.1 fusion.13
  140.2 0.8 fusion.5
  145.1 3.3 slice.201
  148.7 2.6 convolution_add_fusion.residual
  151.8 20.7 %ffn.1 = (bf16[128,1024]{1,0:T(8,128)(2,1)S(1)}, f32[128,1024]{1,0:T(8,128)S(1)}, f32[1,1024]{1,0:T(1,128)S(1)}, bf16[4,4,4,480,128]{4,3,2,1,0:T(8,128)(2,1)}) custom-call(f32[128,1024]{1,0:T(8,128)S(1)} %convolution_add_fusion.residual, f32[1,1024]{1,0:T(1,128)S(1)} %reshape.447.gain, bf16[128,1024]{1,0:T(8,128)(2,1)S(1)} %copy.157.cot, ...), custom_call_target="tpu_custom_call" | custom-call | tf_op jit(solution)/shard_map/ffn/pallas_call | solution.py:627
  173.2 0.7 reshape_reshape.28
  173.9 1.6 multiply_reduce_fusion.3
  176.2 20.3 %while.34 = (s32[]{:T(128)}, f32[128,5,3,64]{0,3,2,1:T(8,128)S(1)}, bf16[4,512,320]{1,2,0:T(8,128)(2,1)}, bf16[4,512,320]{1,2,0:T(8,128)(2,1)}, s32[4]{0:T(128)}...) while((s32[]{:T(128)}, f32[128,5,3,64]{0,3,2,1:T(8,128)S(1)}, ...), condition=%wide.region_15.16_spmd.clone, body=%wide.region_11.15_spmd.clone.sunk | while | flops 639750784 | bytes 22876700 | solution.py:866
  176.2 1.2 dynamic_slice.67
  178.6 6.8 %conditional.7 = (f32[128,5,3,64]{0,3,2,1:T(8,128)S(1)}, bf16[1,512,320]{1,2,0:T(8,128)(2,1)S(1)}, bf16[1,512,320]{1,2,0:T(8,128)(2,1)S(1)}) conditional(s32[]{:T(128)} %convert_element_type.191, f32[128,5,3,64]{0,3,2,1:T(8,128)S(1)} %get-tuple-element.920, (s32[128]{0:T(128)S(1)}, s32[]{:T(128)}, s32[5]{0:T(128)}, s32[]{:T(128)}, ...), branch_computations={%region_12.12_spmd, %region_13.14_spmd} | conditional | flops 639750784 | bytes 21564656 | solution.py:861
  179.7 2.4 fusion.27
  183.4 2.0 fusion.31
  185.4 0.9 constant_dynamic-update-slice_fusion.3
  186.3 1.2 dynamic_slice.67
  188.8 0.9 constant_dynamic-update-slice_fusion.3
  189.7 1.2 dynamic_slice.67
  192.2 0.9 constant_dynamic-update-slice_fusion.3
  193.1 1.2 dynamic_slice.67
  195.6 0.9 constant_dynamic-update-slice_fusion.3
  196.5 2.7 copy.162
  199.2 1.6 copy.163
  200.8 2.9 pad_maximum_fusion.1.terms
  203.6 59.2 %reduce_keys.1 = f32[128,640]{1,0:T(8,128)S(1)} custom-call(bf16[2,4,2,128,640]{4,3,2,1,0:T(8,128)(2,1)S(1)} %pad_maximum_fusion.1.terms), custom_call_target="tpu_custom_call" | custom-call | tf_op jit(solution)/shard_map/reduce_keys/pallas_call | solution.py:520
  263.9 0.8 mul.291
  264.7 1.2 subtract_convert_fusion
  265.9 2.2 fusion.60
  268.2 2.7 multiply_reduce_fusion
  271.6 2.7 concatenate.80
  274.3 3.6 %copy.171 = bf16[2,4,2,64,2,4,128]{6,3,5,0,4,1,2:T(8,128)(2,1)} copy(bf16[2,4,2,64,2,4,128]{6,5,4,3,2,1,0:T(4,128)(2,1)} %concatenate.80) | data formatting | bytes 4194304 | tf_op jit(solution)/shard_map/concatenate | solution.py:896
  278.0 1.7 convolution_convert_fusion.2
  279.7 2.9 concatenate.81
  282.6 1.6 copy.172
  284.9 2.8 concatenate.79
  287.7 3.6 %copy.170 = bf16[2,4,2,64,2,4,128]{6,3,5,0,4,1,2:T(8,128)(2,1)} copy(bf16[2,4,2,64,2,4,128]{6,5,4,3,2,1,0:T(4,128)(2,1)} %concatenate.79) | data formatting | bytes 4194304 | tf_op jit(solution)/shard_map/concatenate | solution.py:896
  291.3 2.6 pad_maximum_fusion
  294.0 55.6 %reduce_grads.1 = (f32[176,128]{1,0:T(8,128)S(1)}, f32[480,128]{1,0:T(8,128)S(1)}, f32[160,128]{1,0:T(8,128)S(1)}, f32[16,128]{1,0:T(8,128)S(1)}) custom-call(bf16[2,4,4,4,176,128]{5,4,3,2,1,0:T(8,128)(2,1)S(1)} %bitcast.234, bf16[4,4,4,480,128]{4,3,2,1,0:T(8,128)(2,1)} %get-tuple-element.372.ffn_terms, f32[16,128]{1,0:T(8,128)S(1)} %pad_maximum_fusion.7.gain_terms), custom_call_target="tpu_custom_call" | custom-call | tf_op jit(solution)/shard_map/reduce_grads/pallas_call | solution.py:354
  349.8 0.8 copy.178
  357.3 0.7 broadcast_in_dim_reshape.7
  358.2 0.7 broadcast_in_dim_reshape.6
  (218 shorter events, 21.7 us)
Async XLA Ops:
  63.7 3.1 copy-start
  72.0 10.4 %copy-start.20 = (bf16[1,128,960]{1,2,0:T(8,128)(2,1)S(1)}, bf16[1,128,960]{1,2,0:T(8,128)(2,1)}, u32[]{:S(2)}) copy-start(bf16[1,128,960]{1,2,0:T(8,128)(2,1)} %param.20) | copy-start | bytes 737284
  72.0 10.6 %copy-start.23 = (f32[960]{0:T(1024)S(1)}, f32[960]{0:T(1024)}, u32[]{:S(2)}) copy-start(f32[960]{0:T(1024)} %param.22) | copy-start | bytes 11524
  82.9 3.0 copy-start.8
  83.0 2.6 copy-start.25
  85.9 2.3 copy-start.18
  144.9 3.5 copy-start.6
  145.1 3.6 copy-start.12
  148.4 2.9 copy-start.21
  148.7 3.0 copy-start.2
  148.7 2.9 copy-start.24
  151.8 20.8 %copy-start.1 = (bf16[16,64,1024]{2,1,0:T(8,128)(2,1)S(1)}, bf16[16,64,1024]{2,1,0:T(8,128)(2,1)}, u32[]{:S(2)}) copy-start(bf16[16,64,1024]{2,1,0:T(8,128)(2,1)} %slice.201) | copy-start | bytes 6291460
  172.5 1.4 copy-start.7
  178.6 0.8 copy-start.26
  178.6 0.9 copy-start.27
  178.6 1.1 copy-start.22
  196.5 2.7 copy-start.17
  203.6 59.4 %copy-start.19 = (f32[128,64]{0,1:T(8,128)S(1)}, f32[128,64]{0,1:T(8,128)}, u32[]{:S(2)}) copy-start(f32[128,64]{0,1:T(8,128)} %copy-done.18) | copy-start | bytes 98308
  263.7 4.5 %copy-start.15 = (bf16[128,16,48]{0,2,1:T(8,128)(2,1)}, bf16[128,16,48]{0,2,1:T(8,128)(2,1)S(1)}, u32[]{:S(2)}) copy-start(bf16[128,16,48]{0,2,1:T(8,128)(2,1)S(1)} %maximum_maximum_fusion) | copy-start | bytes 589828
  263.9 4.3 %copy-start.3 = (f32[128,1024]{1,0:T(8,128)S(1)}, f32[128,1024]{1,0:T(8,128)}, u32[]{:S(2)}) copy-start(f32[128,1024]{1,0:T(8,128)} %copy-done.2) | copy-start | bytes 1572868
  265.9 5.0 %copy-start.10 = (bf16[128,16,60]{0,2,1:T(8,128)(2,1)}, bf16[128,16,60]{0,2,1:T(8,128)(2,1)S(1)}, u32[]{:S(2)}) copy-start(bf16[128,16,60]{0,2,1:T(8,128)(2,1)S(1)} %subtract_convert_fusion) | copy-start | bytes 737284
  265.9 4.9 %copy-start.13 = (bf16[128,16,64]{0,2,1:T(8,128)(2,1)S(1)}, bf16[128,16,64]{0,2,1:T(8,128)(2,1)}, u32[]{:S(2)}) copy-start(bf16[128,16,64]{0,2,1:T(8,128)(2,1)} %copy-done.12) | copy-start | bytes 786436
  274.3 3.6 %copy-start.9 = (bf16[128,16,64]{0,2,1:T(8,128)(2,1)S(1)}, bf16[128,16,64]{0,2,1:T(8,128)(2,1)}, u32[]{:S(2)}) copy-start(bf16[128,16,64]{0,2,1:T(8,128)(2,1)} %copy-done.8) | copy-start | bytes 786436
  274.3 3.6 %copy-start.16 = (bf16[128,16,48]{0,2,1:T(8,128)(2,1)S(1)}, bf16[128,16,48]{0,2,1:T(8,128)(2,1)}, u32[]{:S(2)}) copy-start(bf16[128,16,48]{0,2,1:T(8,128)(2,1)} %copy-done.15) | copy-start | bytes 589828
  279.7 4.5 %copy-start.11 = (bf16[128,16,60]{0,2,1:T(8,128)(2,1)S(1)}, bf16[128,16,60]{0,2,1:T(8,128)(2,1)}, u32[]{:S(2)}) copy-start(bf16[128,16,60]{0,2,1:T(8,128)(2,1)} %copy-done.10) | copy-start | bytes 737284
  287.7 3.6 %copy-start.5 = (bf16[2,4,2,64,2,4,128]{6,3,5,0,4,1,2:T(8,128)(2,1)S(1)}, bf16[2,4,2,64,2,4,128]{6,3,5,0,4,1,2:T(8,128)(2,1)}, u32[]{:S(2)}) copy-start(bf16[2,4,2,64,2,4,128]{6,3,5,0,4,1,2:T(8,128)(2,1)} %copy.171) | copy-start | bytes 6291460
  349.6 7.3 %copy-start.4 = (f32[128,1024]{1,0:T(8,128)S(1)}, f32[128,1024]{1,0:T(8,128)}, u32[]{:S(2)}) copy-start(f32[128,1024]{1,0:T(8,128)} %copy-done.2) | copy-start | bytes 1572868
  349.6 7.3 %copy-start.14 = (f32[128,1024]{1,0:T(8,128)S(1)}, f32[128,1024]{1,0:T(8,128)}, u32[]{:S(2)}) copy-start(f32[128,1024]{1,0:T(8,128)} %get-tuple-element.665) | copy-start | bytes 1572868

commit v2 on v0

v2 whole, which is shorter than its diff:
```python
import functools

import jax
import jax.numpy as jnp
from jax import lax
from jax.experimental import pallas as pl
from jax.experimental.pallas import tpu as pltpu
from jax.sharding import PartitionSpec as P

D = 960
HEADS = 15
KVH = 5
HD = 64
NDOC = 4
KVW = 320
WIDE = 1024
TOK = 128

GROUP = HEADS // KVH
STACK = GROUP * TOK
WIDE_KV = 2 * KVW

epsilon = 1e-05
masked_score = -1e30

MESH = pl.DeviceIdType.MESH
ANY = pl.BlockSpec(memory_space=pl.ANY)
VMEM = pl.BlockSpec(memory_space=pltpu.VMEM)
MIB = 1024 * 1024

ATTN_PARTS = ((0, 64), (64, 64), (128, 48))
ATTN_ROWS = 176
FFN_PARTS = ((0, 160), (160, 160), (320, 160))
FFN_ROWS = 480
ORDERS = ((0, 1, 2), (1, 2, 0), (2, 0, 1))


def place():
    c = lax.axis_index("ctx")
    f = lax.axis_index("fsdp")
    x = lax.rem(lax.div(c, 2), 4)
    y = lax.div(f, 4) * 2 + lax.div(c, 8)
    return (x, y, lax.rem(f, 4)), lax.rem(c, 2)


def device(spot, core):
    x, y, z = spot
    return ((lax.rem(y, 2) * 4 + x) * 2 + core, lax.div(y, 2) * 4 + z)


def ring(value, by):
    return lax.rem(value + by + 4, 4)


def shifted(spot, axis, by):
    return tuple(ring(v, by) if i == axis else v for i, v in enumerate(spot))


def greet(devices):
    barrier = pltpu.get_barrier_semaphore()
    for target in devices:
        pl.semaphore_signal(barrier, inc=1, device_id=target, device_id_type=MESH)
    pl.semaphore_wait(barrier, len(devices))


def remote(src, dst, send, recv, target):
    copy = pltpu.make_async_remote_copy(
        src_ref=src, dst_ref=dst, send_sem=send, recv_sem=recv, device_id=target, device_id_type=MESH
    )
    copy.start()
    return copy


def view(ref, lead, spot, done, axis, position, rows, half=None):
    index = []
    cut = min(done) if (half is not None and done) else None
    for a in range(3):
        if a == cut:
            index.append(pl.ds(2 * half, 2))
        elif a in done:
            index.append(pl.ds(0, 4))
        elif a == axis:
            index.append(position)
        else:
            index.append(spot[a])
    low, count = rows
    if half is not None and not done:
        first = (count // 32) * 16
        low, count = (low, first) if half == 0 else (low + first, count - first)
    return ref.at[tuple(lead) + tuple(index) + (pl.ds(low, count),)]


def add_into(target, terms):
    lead = target.shape[:-2]
    if not lead:
        total = target[...].astype(jnp.float32)
        for term in terms:
            total += term[...].astype(jnp.float32)
        target[...] = total.astype(target.dtype)
        return
    inner = lead[1] if len(lead) == 2 else 1

    def body(i, carry):
        at = (lax.div(i, inner), lax.rem(i, inner)) if len(lead) == 2 else (i,)
        total = target[at].astype(jnp.float32)
        for term in terms:
            total += term[at].astype(jnp.float32)
        target[at] = total.astype(target.dtype)
        return carry

    lax.fori_loop(0, lead[0] * inner, body, 0)


def reduce_shapes(rows):
    count = rows[1]
    first = (count // 32) * 16
    return (
        ((2, 4, count), (4, 4, count)),
        ((2, count), (4, count)),
        ((count - first,), (count,)),
    )


def dot(left, right, left_dim=1, right_dim=0):
    return lax.dot_general(left, right, (((left_dim,), (right_dim,)), ((), ())), preferred_element_type=jnp.float32)


def layer_kernel(
    inputs, doc_offsets, attn_gain_in, ffn_gain_in, query_weight, key_weight, value_weight, proj_weight, gate_weight, up_weight, down_weight, cotangent,
    layer_out, input_grad, query_grad, key_grad, value_grad, proj_grad, gate_grad, up_grad, down_grad, gain_sums,
    attn_w, ffn_w, attn_block, ffn_own, down_away, down_in, pads, wide_in, gain_rows, cosine, sine, segments,
    attn_out, ffn_out, down_out, gain_out,
    normed, normed_t, rows_f32, query_t, query, key_own, keys, scores, mixed, mixed_t, residual,
    tokens, cots, out_sum, norm_sum, out_in, norm_in,
    d_mixed_t, d_mixed, d_query, d_query_t, key_terms, key_pair, key_far, key_near, key_across, d_key_t,
    attn_g, pair_in, gain_slots,
    *scratch,
):
    slots = scratch[:36]
    (
        send, recv, own_sem, down_sem, pair_send, pair_recv,
        key_own_sem, key_send, key_recv, kpair_send, kpair_recv,
        ffn_send, ffn_recv, kg_send, kg_recv, r_send, r_recv, gain_send, gain_recv, last_send, last_recv,
    ) = scratch[36:]
    low = jnp.bfloat16
    spot, core = place()
    x, y, z = spot
    half = lax.rem(y, 2)
    sibling = device(spot, 1 - core)
    across = device((x, y + 1 - 2 * half, z), core)
    chunks = half * 2 + lax.div(x, 2) + 1
    sent = []

    def hot(rows, columns, shift):
        row = lax.broadcasted_iota(jnp.int32, (rows, columns), 0)
        column = lax.broadcasted_iota(jnp.int32, (rows, columns), 1)
        return column == row + shift(row)

    by_sixty = lambda row: lax.shift_right_logical(row * 1093, 16) * 4
    columns_of = hot(120, 128, by_sixty).astype(low)
    zeros = lambda rows: jnp.zeros((rows, 128), jnp.float32)
    turn = lambda ref: dot(ref[...], columns_of)
    attn_block[pl.ds(128, 48)] = jnp.concatenate([turn(key_weight), turn(value_weight), zeros(8)], axis=0).astype(low)
    attn_block[pl.ds(0, 64)] = jnp.concatenate([turn(query_weight), zeros(4)], axis=0).astype(low)
    attn_block[pl.ds(64, 64)] = jnp.concatenate([turn(proj_weight), zeros(4)], axis=0).astype(low)
    ffn_own[pl.ds(0, 160)] = turn(gate_weight).astype(low)
    ffn_own[pl.ds(160, 160)] = turn(up_weight).astype(low)
    placed = hot(60, 128, lambda row: 64 * core).astype(low)
    down_both = dot(down_weight[...], placed, 0, 0)
    down_away[...] = jnp.where(core == 0, down_both[160:], down_both[:160]).astype(low)
    ffn_own[pl.ds(320, 160)] = jnp.where(core == 0, down_both[:160], down_both[160:]).astype(low)

    greet([device(shifted(spot, a, by), core) for a in range(3) for by in (1, 2, 3)] + [sibling])
    down_copy = remote(down_away, down_in, down_sem.at[0], down_sem.at[1], sibling)
    sent.append(down_copy)
    own_attn = pltpu.make_async_copy(attn_block, attn_w.at[core, x, y, z], own_sem.at[0])
    own_attn.start()
    waiting, gathered, paired = {}, [], {}

    def pass_on(part, number, position):
        order = ORDERS[part]
        piece = view(attn_w, (core,), spot, order[:2], order[2], position, ATTN_PARTS[part])
        paired[part, number] = remote(piece, piece, pair_send.at[part, number], pair_recv.at[part, number], sibling)

    def direct(kind, stage):
        return stage < 2 - kind

    def gather_step(kind, stage, second, some=(2, 0, 1)):
        for part in some:
            axis, done = ORDERS[part][stage], ORDERS[part][:stage]
            if kind == 0:
                whole, lead, rows, block = attn_w, (core,), ATTN_PARTS[part], attn_block
            else:
                whole, lead, rows, block = ffn_w, (), FFN_PARTS[part], ffn_own
            for copy in waiting.pop((kind, part), ()):
                copy.wait_recv()
            me = spot[axis]
            copies = []
            for way, by in enumerate((1, -1, 2) if direct(kind, stage) else (1, -1)):
                target = device(shifted(spot, axis, by), core)
                if second:
                    source = goal = view(whole, lead, spot, done, axis, ring(me, -by), rows, half=way)
                else:
                    source = goal = view(whole, lead, spot, done, axis, me, rows)
                    if stage == 0:
                        source = block.at[pl.ds(rows[0], rows[1])]
                copies.append(
                    remote(
                        source, goal,
                        send.at[kind, part, stage, second, way], recv.at[kind, part, stage, second, way], target,
                    )
                )
            waiting[kind, part] = copies
            (sent if kind == 0 else gathered).extend(copies)
            if kind == 0 and stage == 2:
                if second:
                    pass_on(part, 1, ring(me, 1))
                    pass_on(part, 2, ring(me, -1))
                else:
                    pass_on(part, 0, me)

    def settle(kind, part):
        for copy in waiting.pop((kind, part), ()):
            copy.wait_recv()

    gather_step(0, 0, 0)

    def fill_pads(i, carry):
        start = pl.multiple_of(i * 160, 160)
        pads[pl.ds(start, 160)] = hot(160, WIDE, lambda row: start + by_sixty(row + start)).astype(low)
        return carry

    lax.fori_loop(0, 6, fill_pads, 0)
    wide_in[...] = dot(inputs[...], pads[...], 0, 0)
    cots[pl.ds(0, TOK)] = dot(cotangent[...], pads[...], 0, 0).astype(low)
    cot_copy = remote(cots.at[pl.ds(0, TOK)], cots.at[pl.ds(TOK, TOK)], ffn_send.at[0], ffn_recv.at[0], sibling)

    def exact(array, places, dim):
        total = jnp.zeros((), jnp.float32)
        for _ in range(3):
            piece = array.astype(low)
            array = array - piece.astype(jnp.float32)
            total = total + dot(piece, places, 1, dim)
        return total

    gain_rows[...] = exact(
        jnp.concatenate([attn_gain_in[...], ffn_gain_in[...], jnp.zeros((6, D), jnp.float32)], axis=0), pads[...], 0
    )
    attn_gain, ffn_gain = gain_rows[0:1, :], gain_rows[1:2, :]
    down_copy.wait_recv()
    ffn_own[pl.ds(320, 160)] = ffn_own[pl.ds(320, 160)] + down_in[...]
    own_ffn = pltpu.make_async_copy(ffn_own, ffn_w.at[x, y, z], own_sem.at[1])
    own_ffn.start()
    own_attn.wait()
    gather_step(0, 1, 0)
    gather_step(1, 0, 0)
    tok = wide_in[...]
    attn_scale = lax.rsqrt(jnp.sum(tok * tok, axis=-1, keepdims=True) * (1.0 / D) + epsilon)
    wide_normed = tok * attn_scale * attn_gain
    normed[...] = wide_normed.astype(low)
    normed_t[...] = wide_normed.T.astype(low)
    own_ffn.wait()
    gather_step(0, 2, 0)

    first_row = (half * 8 + x * 2 + core) * TOK

    def document(index):
        number, start = jnp.zeros_like(index), jnp.zeros_like(index)
        for i in range(1, NDOC):
            after = index >= doc_offsets[0, i]
            number += jnp.where(after, 1, 0)
            start = jnp.where(after, doc_offsets[0, i], start)
        return number, start

    table_token = first_row + lax.broadcasted_iota(jnp.int32, (HD // 2, TOK), 1)
    row = lax.broadcasted_iota(jnp.int32, (HD // 2, TOK), 0)
    rates = jnp.zeros((HD // 2, TOK), jnp.float32)
    for i in range(HD // 2):
        rates = jnp.where(row == i, 10000.0 ** (-2.0 * i / HD), rates)
    angles = (table_token - document(table_token)[1]).astype(jnp.float32) * rates
    cosine[...] = jnp.cos(angles)
    sine[...] = jnp.sin(angles)
    row = lax.broadcasted_iota(jnp.int32, (16, 512), 0)
    for j in range(4):
        number = document(512 * j + lax.broadcasted_iota(jnp.int32, (16, 512), 1))[0]
        segments[j] = jnp.where(number == row, 1.0, 0.0).astype(low)
    row = lax.broadcasted_iota(jnp.int32, (16, STACK), 0)
    own_token = first_row + jnp.bitwise_and(lax.broadcasted_iota(jnp.int32, (16, STACK), 1), TOK - 1)
    apart = jnp.where((document(own_token)[0] != row) & (row < NDOC), masked_score, 0.0)
    last_key = first_row + jnp.bitwise_and(lax.broadcasted_iota(jnp.int32, (STACK, 512), 0), TOK - 1)

    gather_step(0, 2, 1)
    gather_step(1, 1, 0)
    for part in (2, 0, 1):
        settle(0, part)
        pass_on(part, 3, ring(spot[ORDERS[part][2]], 2))
    sent.extend(paired.values())

    def settle_pairs(part):
        for number in range(4):
            paired[part, number].wait_recv()

    def weight_rows(where, rows):
        y_lo, p = where
        return jnp.concatenate(
            [
                jnp.concatenate([attn_w[p, i, 2 * (f // 4) + y_lo, f % 4, rows] for f in range(8)], axis=1)
                for i in range(4)
            ],
            axis=0,
        )

    groups = [(y_lo, p) for y_lo in (0, 1) for p in (0, 1)]

    def shard(where, i):
        return (where[0] * 4 + i) * 2 + where[1]

    def turned(v1, v2, back):
        c, s = cosine[...], (-sine[...] if back else sine[...])
        return v1 * c - v2 * s, v2 * c + v1 * s

    settle_pairs(2)
    for where in groups:
        term = dot(weight_rows(where, pl.ds(128, 48)), normed_t[...])
        for i in range(4):
            c = shard(where, i)
            rows_f32[pl.ds(20 * c, 20)] = term[48 * i : 48 * i + 20]
            rows_f32[pl.ds(KVW + 20 * c, 20)] = term[48 * i + 20 : 48 * i + 40]
    for h in range(KVH):
        v1, v2 = turned(rows_f32[pl.ds(64 * h, 32)], rows_f32[pl.ds(64 * h + 32, 32)], False)
        key_own[pl.ds(64 * h, 32)] = v1.astype(low)
        key_own[pl.ds(64 * h + 32, 32)] = v2.astype(low)
    key_own[pl.ds(KVW, KVW)] = rows_f32[pl.ds(KVW, KVW)].astype(low)

    mine = keys.at[half, x, core]
    own_keys = pltpu.make_async_copy(key_own, mine, key_own_sem)
    own_keys.start()
    kpairs = []

    def pass_keys(ref):
        kpairs.append(remote(ref, ref, kpair_send.at[len(kpairs)], kpair_recv.at[len(kpairs)], sibling))

    def key_copy(source, goal, number, target):
        return remote(source, goal, key_send.at[number], key_recv.at[number], target)

    neighbours = [device(shifted(spot, 0, by), core) for by in (1, -1)]
    over = key_copy(key_own, mine, 0, across)
    first = [key_copy(key_own, mine, 1 + way, neighbours[way]) for way in (0, 1)]
    kpairs.append(remote(key_own, mine, kpair_send.at[0], kpair_recv.at[0], sibling))

    gather_step(1, 1, 1)
    settle_pairs(0)
    for where in groups:
        term = dot(weight_rows(where, pl.ds(0, 64)), normed_t[...])
        for i in range(4):
            rows_f32[pl.ds(60 * shard(where, i), 60)] = term[64 * i : 64 * i + 60]

    over.wait_recv()
    other = keys.at[1 - half, x, core]
    second = [key_copy(other, other, 3 + way, neighbours[way]) for way in (0, 1)]
    pass_keys(other)

    def heads(h, carry):
        pieces = []
        for g in range(GROUP):
            at = pl.multiple_of((h * GROUP + g) * HD, HD)
            v1, v2 = turned(rows_f32[pl.ds(at, 32)], rows_f32[pl.ds(pl.multiple_of(at + 32, 32), 32)], False)
            pieces.append(jnp.concatenate([v1, v2], axis=0) * (HD ** -0.5))
        wide = jnp.concatenate(pieces, axis=1)
        query_t[h] = wide.astype(low)
        query[h] = jnp.concatenate([wide, apart], axis=0).T.astype(low)
        return carry

    lax.fori_loop(0, KVH, heads, 0)
    gather_step(1, 2, 0, (0,))

    last = []
    for way, by in enumerate((1, -1)):
        first[way].wait_recv()
        ref = keys.at[half, ring(x, -by), core]
        if way == 0:
            last.append(key_copy(ref, ref, 5, neighbours[0]))
        pass_keys(ref)
    for way, by in enumerate((1, -1)):
        second[way].wait_recv()
        ref = keys.at[1 - half, ring(x, -by), core]
        if way == 1:
            last.append(key_copy(ref, ref, 6, neighbours[1]))
        pass_keys(ref)
    gather_step(1, 2, 0, (1, 2))
    for h in (0, 1):
        last[h].wait_recv()
        pass_keys(keys.at[(half, 1 - half)[h], ring(x, 2), core])
    own_keys.wait()
    for copy in kpairs:
        copy.wait_recv()
    sent.extend([over] + first + second + last + kpairs)

    def key_chunk(j, at):
        rows = pl.ds(pl.multiple_of(at, HD), HD)
        y_lo, i = lax.div(j, 2), 2 * lax.rem(j, 2)
        return jnp.concatenate([keys[y_lo, i + n // 2, n % 2, rows, :] for n in range(4)], axis=1)

    def block_scores(h, j, newest):
        block = dot(query[h], jnp.concatenate([key_chunk(j, h * HD), segments[j]], axis=0))
        if newest:
            index = j * 512 + lax.broadcasted_iota(jnp.int32, (STACK, 512), 1)
            block = jnp.where(index <= last_key, block, masked_score)
        return block

    def quarters(block, joined):
        return joined(
            joined(block[:, :128], block[:, 128:256]), joined(block[:, 256:384], block[:, 384:])
        )

    def forward_head(h, carry):
        def tops(newest, j, top):
            block = block_scores(h, j, newest)
            scores[j] = block
            return jnp.maximum(top, quarters(block, jnp.maximum))

        top = tops(True, chunks - 1, jnp.full((STACK, 128), masked_score, jnp.float32))
        top = lax.fori_loop(0, chunks - 1, functools.partial(tops, False), top)
        top = jnp.max(top, axis=1, keepdims=True)
        mixed[h, :, :HD] = jnp.zeros((STACK, HD), jnp.float32)

        def weigh(j, total):
            raised = jnp.exp(scores[j] - top)
            mixed[h, :, :HD] += dot(raised.astype(low), key_chunk(j, KVW + h * HD), 1, 1)
            return total + quarters(raised, jnp.add)

        total = lax.fori_loop(0, chunks, weigh, jnp.zeros((STACK, 128), jnp.float32))
        total = jnp.sum(total, axis=1, keepdims=True)
        mixed[h, :, HD : HD + 1] = top + jnp.log(total)
        out = mixed[h, :, :HD] / total
        mixed[h, :, :HD] = out
        out_t = out.T
        for g in range(GROUP):
            rows_f32[pl.ds(pl.multiple_of((h * GROUP + g) * HD, HD), HD)] = out_t[:, 128 * g : 128 * g + 128]
        return carry

    lax.fori_loop(0, 3, forward_head, 0)
    gather_step(1, 2, 1)
    lax.fori_loop(3, 5, forward_head, 0)

    def widen(goal):
        for c in range(16):
            piece = jnp.concatenate([rows_f32[pl.ds(60 * c, 60)], jnp.zeros((4, TOK), jnp.float32)], axis=0)
            goal[pl.ds(64 * c, 64)] = piece.astype(low)

    widen(mixed_t)
    settle_pairs(1)
    for where in groups:
        term = dot(weight_rows(where, pl.ds(64, 64)), mixed_t[...])
        for i in range(4):
            rows_f32[pl.ds(64 * shard(where, i), 64)] = term[64 * i : 64 * i + 64]
    residual[...] = wide_in[...] + rows_f32[...].T

    res = residual[...]
    ffn_scale = lax.rsqrt(jnp.sum(res * res, axis=-1, keepdims=True) * (1.0 / D) + epsilon)
    tokens[pl.ds(0, TOK)] = (res * ffn_scale * ffn_gain).astype(low)
    token_copy = remote(tokens.at[pl.ds(0, TOK)], tokens.at[pl.ds(TOK, TOK)], ffn_send.at[1], ffn_recv.at[1], sibling)
    out_sum[...] = jnp.zeros_like(out_sum)
    norm_sum[...] = jnp.zeros_like(norm_sum)
    cot_copy.wait_recv()
    for part in (0, 1, 2):
        settle(1, part)
    for copy in gathered:
        copy.wait_send()
    token_copy.wait_recv()

    def ffn_at(part, block, lane):
        high, slow = lax.div(block, 4), lax.rem(block, 4)
        if part == 2:
            return (lane % 4, high * 2 + lane // 4, slow, pl.ds(320, 160))
        return (slow, (lane // 4) * 2 + high, lane % 4, pl.ds(160 * part, 160))

    def ffn_chunk(j, carry):
        gate_rows, up_rows, down_rows = [
            jnp.concatenate(
                [
                    jnp.concatenate([ffn_w[ffn_at(part, 2 * j + u, lane)] for lane in range(8)], axis=1)
                    for u in (0, 1)
                ],
                axis=0,
            )
            for part in (0, 1, 2)
        ]
        both, cot_both = tokens[...], cots[...]
        gate_value = dot(both, gate_rows, 1, 1)
        up_value = dot(both, up_rows, 1, 1)
        d_hidden = dot(cot_both, down_rows, 1, 1)
        sigmoid = 1.0 / (1.0 + jnp.exp(-gate_value))
        silu = gate_value * sigmoid
        hidden = (silu * up_value).astype(low)
        d_gate = (d_hidden * up_value * sigmoid * (1.0 + gate_value * (1.0 - sigmoid))).astype(low)
        d_up = (d_hidden * silu).astype(low)
        out_sum[...] += dot(hidden, down_rows)
        norm_sum[...] += dot(d_gate, gate_rows) + dot(d_up, up_rows)
        for part, (left, right) in enumerate(((d_gate, both), (d_up, both), (hidden, cot_both))):
            term = dot(left, right, 0, 0).astype(low)
            for u in (0, 1):
                for lane in range(8):
                    ffn_w[ffn_at(part, 2 * j + u, lane)] = term[160 * u : 160 * u + 160, 128 * lane : 128 * lane + 128]
        return carry

    lax.fori_loop(0, 4, ffn_chunk, 0)
    theirs = pl.ds(TOK, TOK)
    norm_copy = remote(norm_sum.at[theirs], norm_in, ffn_send.at[2], ffn_recv.at[2], sibling)
    out_copy = remote(out_sum.at[theirs], out_in, ffn_send.at[3], ffn_recv.at[3], sibling)
    sent.extend([cot_copy, token_copy, norm_copy, out_copy])

    def slot(kind, part, stage, second, way):
        ref = slots[((kind * 3 + part) * 3 + stage) * 2 + second]
        return ref.at[way]

    def reduce_step(kind, stage, second, some=(0, 1, 2)):
        whole, lead, parts = (attn_g, (core,), ATTN_PARTS) if kind == 0 else (ffn_w, (), FFN_PARTS)
        for part in some:
            rows = parts[part]
            if stage < 3:
                axis, done = ORDERS[part][2 - stage], ORDERS[part][: 2 - stage]
            arrived = waiting.pop((2 + kind, part), ())
            for copy in arrived:
                copy.wait_recv()
            if arrived and not second:
                before, full = ORDERS[part][3 - stage], ORDERS[part][: 3 - stage]
                add_into(
                    view(whole, lead, spot, full, before, spot[before], rows),
                    [slot(kind, part, stage - 1, 1, way) for way in range(3 if direct(kind, 3 - stage) else 2)],
                )
            if stage == 3:
                goal = attn_out if kind == 0 else ffn_out
                goal[pl.ds(rows[0], rows[1])] = whole[lead + spot + (pl.ds(rows[0], rows[1]),)].astype(jnp.float32)
                continue
            straight = direct(kind, 2 - stage)
            me = spot[axis]
            copies = []
            for way, by in enumerate((1, -1, 2) if straight else (1, -1)):
                target = device(shifted(spot, axis, by), core)
                if straight:
                    source = view(whole, lead, spot, done, axis, ring(me, by), rows)
                elif second:
                    add_into(
                        view(whole, lead, spot, done, axis, ring(me, by), rows, half=way),
                        [slot(kind, part, stage, 0, way)],
                    )
                    source = view(whole, lead, spot, done, axis, ring(me, by), rows)
                else:
                    source = view(whole, lead, spot, done, axis, ring(me, 2), rows, half=way)
                copies.append(
                    remote(
                        source, slot(kind, part, stage, 1 if straight else second, way),
                        r_send.at[kind, part, stage, second, way], r_recv.at[kind, part, stage, second, way], target,
                    )
                )
            waiting[2 + kind, part] = copies
            sent.extend(copies)

    reduce_step(1, 0, 0)
    norm_copy.wait_recv()
    d_normed = norm_sum[pl.ds(0, TOK)] + norm_in[...]
    res = residual[...]
    ffn_scale = lax.rsqrt(jnp.sum(res * res, axis=-1, keepdims=True) * (1.0 / D) + epsilon)
    ffn_gain_term = jnp.sum(d_normed * res * ffn_scale, axis=0, keepdims=True)
    gain_out[...] = exact(jnp.concatenate([jnp.zeros_like(ffn_gain_term), ffn_gain_term, jnp.zeros((6, WIDE), jnp.float32)], axis=0), pads[...], 1)
    scaled = d_normed * ffn_gain
    d_residual = cots[pl.ds(0, TOK)].astype(jnp.float32) + ffn_scale * (
        scaled - res * ffn_scale * ffn_scale * (jnp.sum(scaled * res, axis=-1, keepdims=True) * (1.0 / D))
    )
    out_copy.wait_recv()
    layer_out[...] = dot(
        pads[...], (res + out_sum[pl.ds(0, TOK)] + out_in[...]).astype(low), 1, 1
    ).astype(low)
    residual[...] = d_residual
    d_branch = d_residual.astype(low)
    d_branch_t = d_residual.T.astype(low)

    norm_sum[pl.ds(0, TOK)] = jnp.zeros((TOK, WIDE), jnp.float32)
    for where in groups:
        picked = jnp.concatenate(
            [d_branch[:, 64 * shard(where, i) : 64 * shard(where, i) + 64] for i in range(4)], axis=1
        )
        norm_sum[pl.ds(0, TOK)] += dot(picked, weight_rows(where, pl.ds(64, 64)))
    d_wide = norm_sum[pl.ds(0, TOK)].T
    for c in range(16):
        rows_f32[pl.ds(60 * c, 60)] = d_wide[64 * c : 64 * c + 60]

    def attn_grad(left_t, right, offset, count, width):
        for where in groups:
            term = dot(
                jnp.concatenate([left_t[width * shard(where, i) : width * shard(where, i) + width] for i in range(4)], axis=0),
                right,
            ).astype(low)
            y_lo, p = where
            for i in range(4):
                for f in range(8):
                    attn_g[p, i, 2 * (f // 4) + y_lo, f % 4, pl.ds(offset, count)] = term[
                        width * i : width * i + count, 128 * f : 128 * f + 128
                    ]

    gpairs = []

    def share(part):
        rows = pl.ds(*ATTN_PARTS[part])
        gpairs.append(
            remote(
                attn_g.at[1 - core, :, :, :, rows], pair_in.at[:, :, :, rows], last_send.at[part], last_recv.at[part], sibling
            )
        )

    def shared(part):
        rows = pl.ds(*ATTN_PARTS[part])
        gpairs[0].wait_recv()
        sent.append(gpairs.pop(0))

        def body(i, carry):
            at = (lax.div(i, 16), lax.rem(lax.div(i, 4), 4), lax.rem(i, 4), rows)
            goal = (core,) + at
            attn_g[goal] = (attn_g[goal].astype(jnp.float32) + pair_in[at].astype(jnp.float32)).astype(low)
            return carry

        lax.fori_loop(0, 64, body, 0)

    def d_heads(h, carry):
        pieces = [rows_f32[pl.ds(pl.multiple_of((h * GROUP + g) * HD, HD), HD)] for g in range(GROUP)]
        wide = jnp.concatenate(pieces, axis=1)
        d_mixed_t[h] = wide.astype(low)
        d_mixed[h] = wide.T.astype(low)
        return carry

    lax.fori_loop(0, KVH, d_heads, 0)
    mixed_rows = mixed_t[...].astype(jnp.float32).T.astype(low)
    attn_grad(d_branch_t, mixed_rows, 64, 64, 64)
    share(1)
    reduce_step(1, 0, 1)

    def clear(j, carry):
        key_terms[lax.div(j, 4), lax.rem(j, 4)] = jnp.zeros((2, WIDE_KV, TOK), low)
        return carry

    lax.fori_loop(2 * chunks, 8, clear, 0)

    def backward_head(h, carry):
        delta = jnp.sum(d_mixed[h].astype(jnp.float32) * mixed[h, :, :HD], axis=1, keepdims=True)
        d_query[...] = jnp.zeros_like(d_query)

        def visit(newest, j, inner):
            shares = jnp.exp(block_scores(h, j, newest) - mixed[h, :, HD : HD + 1])
            d_shares = dot(d_mixed[h], key_chunk(j, KVW + h * HD))
            d_scores = (shares * (d_shares - delta)).astype(low)
            d_query[...] += dot(d_scores, key_chunk(j, h * HD), 1, 1)
            d_key = dot(query_t[h], d_scores).astype(low)
            d_value = dot(d_mixed_t[h], shares.astype(low)).astype(low)
            y_lo, i = lax.div(j, 2), 2 * lax.rem(j, 2)
            key_rows = pl.ds(pl.multiple_of(h * HD, HD), HD)
            value_rows = pl.ds(pl.multiple_of(KVW + h * HD, HD), HD)
            for n in range(4):
                key_terms[y_lo, i + n // 2, n % 2, key_rows] = d_key[:, 128 * n : 128 * n + 128]
                key_terms[y_lo, i + n // 2, n % 2, value_rows] = d_value[:, 128 * n : 128 * n + 128]
            return inner

        visit(True, chunks - 1, 0)
        lax.fori_loop(0, chunks - 1, functools.partial(visit, False), 0)
        d_wide = d_query[...].T * (HD ** -0.5)
        for g in range(GROUP):
            at = pl.multiple_of((h * GROUP + g) * HD, HD)
            v1, v2 = turned(d_wide[:32, 128 * g : 128 * g + 128], d_wide[32:, 128 * g : 128 * g + 128], True)
            rows_f32[pl.ds(at, 32)] = v1
            rows_f32[pl.ds(pl.multiple_of(at + 32, 32), 32)] = v2
        return carry

    lax.fori_loop(0, 2, backward_head, 0)
    shared(1)
    reduce_step(0, 0, 0, (1,))
    lax.fori_loop(2, 5, backward_head, 0)

    copies = []

    def kg(source, goal, target):
        number = len(copies)
        copies.append(remote(source, goal, kg_send.at[number], kg_recv.at[number], target))
        return copies[-1]

    for by in (2, 1, 3, 0):
        for h in (0, 1):
            kg(key_terms.at[h, ring(x, by), 1 - core], key_pair.at[h, ring(x, by)], sibling)

    def add(goal, *sources):
        total = goal[...].astype(jnp.float32)
        for source in sources:
            total += source[...].astype(jnp.float32)
        goal[...] = total.astype(low)

    def block(h, at):
        return key_terms.at[h, at, core]

    widen(d_query_t)
    attn_grad(d_query_t[...], normed[...], 0, 64, 64)
    share(0)
    reduce_step(1, 1, 0)
    for h in (0, 1):
        copies[h].wait_recv()
        add(block(h, ring(x, 2)), key_pair.at[h, ring(x, 2)])
    far = [kg(block(way, ring(x, 2)), key_far.at[way], neighbours[way]) for way in (0, 1)]
    for copy in copies[2:8]:
        copy.wait_recv()
    for by in (1, 3, 0):
        for h in (0, 1):
            add(block(h, ring(x, by)), key_pair.at[h, ring(x, by)])
    near = []
    for way, by in enumerate((1, -1)):
        far[way].wait_recv()
        add(block(way, ring(x, by)), key_far.at[way])
        near.append(kg(key_terms.at[:, ring(x, by), core], key_near.at[way], neighbours[way]))
    reduce_step(1, 1, 1)
    reduce_step(0, 0, 1, (1,))
    shared(0)
    reduce_step(0, 0, 0, (0,))
    for copy in near:
        copy.wait_recv()
    add(block(1 - half, x), key_near.at[0, 1 - half], key_near.at[1, 1 - half])
    final = kg(block(1 - half, x), key_across, across)
    add(block(half, x), key_near.at[0, half], key_near.at[1, half])
    reduce_step(1, 2, 0)
    norm_sum[pl.ds(0, TOK)] = jnp.zeros((TOK, WIDE), jnp.float32)

    def back_through(left_t, width, offset):
        for where in groups:
            picked = jnp.concatenate(
                [left_t[width * shard(where, i) : width * shard(where, i) + width] for i in range(4)], axis=0
            )
            norm_sum[pl.ds(0, TOK)] += dot(picked, weight_rows(where, pl.ds(offset, width)), 0, 0)

    back_through(d_query_t[...], 64, 0)
    final.wait_recv()
    sent.extend(copies)
    rows_f32[pl.ds(0, WIDE_KV)] = key_terms[half, x, core].astype(jnp.float32) + key_across[...].astype(jnp.float32)
    for h in range(KVH):
        v1, v2 = turned(rows_f32[pl.ds(64 * h, 32)], rows_f32[pl.ds(64 * h + 32, 32)], True)
        rows_f32[pl.ds(64 * h, 32)] = v1
        rows_f32[pl.ds(64 * h + 32, 32)] = v2
    for c in range(16):
        d_key_t[pl.ds(48 * c, 48)] = jnp.concatenate(
            [
                rows_f32[pl.ds(20 * c, 20)],
                rows_f32[pl.ds(KVW + 20 * c, 20)],
                jnp.zeros((8, TOK), jnp.float32),
            ],
            axis=0,
        ).astype(low)
    attn_grad(d_key_t[...], normed[...], 128, 48, 48)
    share(2)
    back_through(d_key_t[...], 48, 128)
    d_normed = norm_sum[pl.ds(0, TOK)]
    tok = wide_in[...]
    attn_scale = lax.rsqrt(jnp.sum(tok * tok, axis=-1, keepdims=True) * (1.0 / D) + epsilon)
    attn_gain_term = jnp.sum(d_normed * tok * attn_scale, axis=0, keepdims=True)
    gain_out[...] = gain_out[...] + exact(
        jnp.concatenate([attn_gain_term, jnp.zeros((7, WIDE), jnp.float32)], axis=0), pads[...], 1
    )

    def gain_start(axis):
        me = spot[axis]
        gain_slots[axis, me] = gain_out[...]
        own = gain_slots.at[axis, me]
        return [
            remote(own, own, gain_send.at[axis, by - 1], gain_recv.at[axis, by - 1], device(shifted(spot, axis, by), core))
            for by in (1, 2, 3)
        ]

    def gain_end(axis, started):
        for copy in started:
            copy.wait_recv()
        sent.extend(started)
        gain_out[...] = (gain_slots[axis, 0] + gain_slots[axis, 1]) + (gain_slots[axis, 2] + gain_slots[axis, 3])

    gains = gain_start(0)
    shared(2)
    reduce_step(0, 0, 0, (2,))
    reduce_step(0, 0, 1, (0,))
    reduce_step(0, 1, 0, (1,))
    gain_end(0, gains)
    gains = gain_start(1)
    reduce_step(0, 0, 1, (2,))
    scaled = d_normed * attn_gain
    d_input = residual[...] + attn_scale * (
        scaled - tok * attn_scale * attn_scale * (jnp.sum(scaled * tok, axis=-1, keepdims=True) * (1.0 / D))
    )
    input_grad[...] = dot(pads[...], d_input.astype(low), 1, 1).astype(low)
    reduce_step(0, 1, 0, (0,))
    reduce_step(0, 2, 0, (1,))
    gain_end(1, gains)
    gains = gain_start(2)
    reduce_step(0, 1, 0, (2,))
    reduce_step(1, 3, 0)
    down_back = remote(ffn_out.at[pl.ds(320, 160)], down_out, down_sem.at[2], down_sem.at[3], sibling)
    sent.append(down_back)
    reduce_step(0, 2, 0, (0,))

    def narrow(ref, low_row, rows):
        return exact(ref[pl.ds(low_row, rows)], columns_of, 1)

    gain_end(2, gains)
    gain_slots[3, core] = gain_out[...]
    own = gain_slots.at[3, core]
    joined = remote(own, own, last_send.at[3], last_recv.at[3], sibling)
    sent.append(joined)
    gate_grad[...] = narrow(ffn_out, 0, 160)
    up_grad[...] = narrow(ffn_out, 160, 160)
    reduce_step(0, 2, 0, (2,))
    reduce_step(0, 3, 0, (1, 0))
    query_grad[...] = narrow(attn_out, 0, 64)[:60]
    proj_grad[...] = narrow(attn_out, 64, 64)[:60]
    down_back.wait_recv()
    mine_down, their_down = ffn_out[pl.ds(320, 160)], down_out[...]
    all_down = jnp.concatenate(
        [jnp.where(core == 0, mine_down, their_down), jnp.where(core == 0, their_down, mine_down)], axis=0
    ).T
    down_grad[...] = jnp.where(core == 0, all_down[:64], all_down[64:])[:60]
    joined.wait_recv()
    gain_sums[...] = gain_slots[3, 0] + gain_slots[3, 1]
    reduce_step(0, 3, 0, (2,))
    both_grads = narrow(attn_out, 128, 48)
    key_grad[...] = both_grads[:20]
    value_grad[...] = both_grads[20:40]
    for copy in sent:
        copy.wait_send()


def run_layer(*operands):
    low, wide = jnp.bfloat16, jnp.float32
    slots = []
    for kind, parts in enumerate((ATTN_PARTS, FFN_PARTS)):
        for rows in parts:
            for stage, (half, full) in enumerate(reduce_shapes(rows)):
                if 2 - stage < 2 - kind:
                    slots += [pltpu.VMEM((16, 128), low), pltpu.VMEM((3,) + full + (128,), low)]
                else:
                    slots += [pltpu.VMEM((2,) + half + (128,), low), pltpu.VMEM((2,) + full + (128,), low)]
    dma = pltpu.SemaphoreType.DMA
    return pl.pallas_call(
        layer_kernel,
        out_shape=[jax.ShapeDtypeStruct((D, TOK), low)] * 2
        + [
            jax.ShapeDtypeStruct(shape, wide)
            for shape in ((60, 120), (20, 120), (20, 120), (60, 120), (160, 120), (160, 120), (60, 320), (8, D))
        ],
        in_specs=[pl.BlockSpec(memory_space=pltpu.SMEM) if i == 1 else VMEM for i in range(len(operands))],
        out_specs=[VMEM] * 10,
        scratch_shapes=[
            pltpu.VMEM((2, 4, 4, 4, ATTN_ROWS, 128), low),
            pltpu.VMEM((4, 4, 4, FFN_ROWS, 128), low),
            pltpu.VMEM((ATTN_ROWS, 128), low),
            pltpu.VMEM((FFN_ROWS, 128), low),
            pltpu.VMEM((160, 128), low),
            pltpu.VMEM((160, 128), low),
            pltpu.VMEM((D, WIDE), low),
            pltpu.VMEM((TOK, WIDE), wide),
            pltpu.VMEM((8, WIDE), wide),
            pltpu.VMEM((HD // 2, TOK), wide),
            pltpu.VMEM((HD // 2, TOK), wide),
            pltpu.VMEM((4, 16, 512), low),
            pltpu.VMEM((ATTN_ROWS, 128), wide),
            pltpu.VMEM((FFN_ROWS, 128), wide),
            pltpu.VMEM((160, 128), wide),
            pltpu.VMEM((8, D), wide),
            pltpu.VMEM((TOK, WIDE), low),
            pltpu.VMEM((WIDE, TOK), low),
            pltpu.VMEM((WIDE, TOK), wide),
            pltpu.VMEM((KVH, HD, STACK), low),
            pltpu.VMEM((KVH, STACK, HD + 16), low),
            pltpu.VMEM((WIDE_KV, TOK), low),
            pltpu.VMEM((2, 4, 2, WIDE_KV, TOK), low),
            pltpu.VMEM((4, STACK, 512), wide),
            pltpu.VMEM((KVH, STACK, 128), wide),
            pltpu.VMEM((WIDE, TOK), low),
            pltpu.VMEM((TOK, WIDE), wide),
            pltpu.VMEM((2 * TOK, WIDE), low),
            pltpu.VMEM((2 * TOK, WIDE), low),
            pltpu.VMEM((2 * TOK, WIDE), wide),
            pltpu.VMEM((2 * TOK, WIDE), wide),
            pltpu.VMEM((TOK, WIDE), wide),
            pltpu.VMEM((TOK, WIDE), wide),
            pltpu.VMEM((KVH, HD, STACK), low),
            pltpu.VMEM((KVH, STACK, HD), low),
            pltpu.VMEM((STACK, HD), wide),
            pltpu.VMEM((WIDE, TOK), low),
            pltpu.VMEM((2, 4, 2, WIDE_KV, TOK), low),
            pltpu.VMEM((2, 4, WIDE_KV, TOK), low),
            pltpu.VMEM((2, WIDE_KV, TOK), low),
            pltpu.VMEM((2, 2, WIDE_KV, TOK), low),
            pltpu.VMEM((WIDE_KV, TOK), low),
            pltpu.VMEM((768, TOK), low),
            pltpu.VMEM((2, 4, 4, 4, ATTN_ROWS, 128), low),
            pltpu.VMEM((4, 4, 4, ATTN_ROWS, 128), low),
            pltpu.VMEM((4, 4, 8, D), wide),
        ]
        + slots
        + [
            dma((2, 3, 3, 2, 3)),
            dma((2, 3, 3, 2, 3)),
            dma((2,)),
            dma((4,)),
            dma((3, 4)),
            dma((3, 4)),
            dma,
            dma((7,)),
            dma((7,)),
            dma((8,)),
            dma((8,)),
            dma((4,)),
            dma((4,)),
            dma((13,)),
            dma((13,)),
            dma((2, 3, 3, 2, 3)),
            dma((2, 3, 3, 2, 3)),
            dma((3, 3)),
            dma((3, 3)),
            dma((4,)),
            dma((4,)),
        ],
        compiler_params=pltpu.CompilerParams(collective_id=1, has_side_effects=True, vmem_limit_bytes=63 * MIB),
        name="layer",
    )(*operands)


def deliver_kernel(count, *refs):
    for i in range(count):
        refs[count + 1 + i][...] = refs[i][...]
    for i in (0, 1):
        refs[2 * count + 1 + i][...] = refs[count][i : i + 1, :]


def deliver(arrays, gains):
    count = len(arrays)
    return pl.pallas_call(
        functools.partial(deliver_kernel, count),
        out_shape=[jax.ShapeDtypeStruct(a.shape, a.dtype) for a in arrays] + [jax.ShapeDtypeStruct((1, D), gains.dtype)] * 2,
        in_specs=[VMEM] * (count + 1),
        out_specs=[VMEM] * (count + 2),
        name="deliver",
    )(*arrays, gains)


def per_device(
    inputs, doc_offsets, attn_gain, query_weight, key_weight, value_weight, proj_weight,
    ffn_gain, gate_weight, up_weight, down_weight, cotangent,
):
    *results, gain_sums = run_layer(
        inputs[0].T, doc_offsets, attn_gain[None], ffn_gain[None], query_weight.T, key_weight.T, value_weight.T,
        proj_weight.T, gate_weight.T, up_weight.T, down_weight.T, cotangent[0].T,
    )
    layer_out, input_grad, query_g, key_g, value_g, proj_g, gate_g, up_g, down_g, attn_gain_g, ffn_gain_g = deliver(
        results, gain_sums
    )
    return (
        layer_out.T[None], input_grad.T[None], attn_gain_g[0], query_g.T, key_g.T, value_g.T, proj_g.T,
        ffn_gain_g[0], gate_g.T, up_g.T, down_g.T,
    )


def solution(mesh):
    split = P("fsdp", "ctx")
    rows = P("fsdp", "ctx", None)
    return jax.shard_map(
        per_device,
        mesh=mesh,
        in_specs=(rows, P("fsdp", None), P(), split, split, split, split, P(), split, split, split, rows),
        out_specs=(rows, rows, P(), split, split, split, split, P(), split, split, split),
        check_vma=False,
    )
```

time: 1080 us -> 160 us (0.15)
  blocking collectives: 450 us -> 0 us
  waiting for transfers between devices: 431 us -> 0 us
  Pallas kernels: 0 us -> 159 us
  local copies, waits for them, and re-layouts: 71.3 us -> 0 us
  matrix products: 60.4 us -> 0 us
  starting transfers between devices: 23.4 us -> 0 us
  between operations: 16.8 us -> 0.78 us
  other arithmetic: 13.4 us -> 0 us
    unnamed x32 -> x0, waiting for transfers between devices: 420 us -> none
    all_gather x9 -> x0, blocking collectives: 284 us -> none  [the longest x1 36.1 us: gather_weights(): lax.all_gather(key_weight, 'fsdp', axis=0, tiled=True)]
    pallas_call x0 -> x2, Pallas kernels: none -> 159 us  [the longest x1 157 us: run_layer(): pl.pallas_call(layer_kernel, out_shape=[jax.ShapeDtypeStruct((D, TOK), lo...]
    unnamed x1 -> x0, blocking collectives: 97.2 us -> none
    psum x1 -> x0, blocking collectives: 68.6 us -> none  [per_device(): gain_totals = lax.psum((attn_gain_term, ffn_gain_term), ('ctx', 'fsdp'))]
    dot_general x28 -> x0, matrix products: 60.4 us -> none  [the longest x7 17.9 us: inner_rows(): lax.dot_general(left, right, (((0,), (0,)), ((), ())), preferred_element_...]
    unnamed x126 -> x0, local copies, waits for them, and re-layouts: 48.6 us -> none
    unnamed x16 -> x0, starting transfers between devices: 23 us -> none
  transfers between devices with their start and end apart: 25 -> 0, of which waited for: 8 -> 0; matrix products, arithmetic and copies ran while one was open for 19% -> 0% of each run, Pallas kernels for 0% -> 0%
where the time goes in v2:
time: 160 us
  Pallas kernels  159 us (99%)
    pallas_call x1, Pallas kernels, run_layer(): pl.pallas_call(layer_kernel, out_shape=[jax.ShapeDtypeStruct((D, TOK), lo...  157 us

profile of v2, /device:TPU:0, one launch (start us, length us, event | category | flops | bytes accessed | tf_op | source)
XLA Modules:
  0.0 160.0 jit_solution(17728866875572064843)
XLA Ops:
  0.6 157.1 %layer.1 = (bf16[960,128]{1,0:T(8,128)(2,1)}, bf16[960,128]{1,0:T(8,128)(2,1)}, f32[60,120]{1,0:T(8,128)}, f32[20,120]{1,0:T(8,128)}, f32[20,120]{1,0:T(8,128)},...) custom-call(bf16[960,128]{1,0:T(8,128)(2,1)} %bitcast.30, ...), custom_call_target="tpu_custom_call" | custom-call | tf_op jit(solution)/shard_map/layer/pallas_call | solution.py:842
  157.7 2.2 %deliver.1 = (bf16[960,128]{1,0:T(8,128)(2,1)}, bf16[960,128]{1,0:T(8,128)(2,1)}, f32[60,120]{1,0:T(8,128)}, f32[20,120]{1,0:T(8,128)}, f32[20,120]{1,0:T(8,128)...) custom-call(bf16[960,128]{1,0:T(8,128)(2,1)} %get-tuple-element.32.r, ...), custom_call_target="tpu_custom_call" | custom-call | tf_op jit(solution)/shard_map/deliver/pallas_call | solution.py:937

commit v3 on v2

--- a/solution.py
+++ b/solution.py
@@ -261,6 +261,7 @@
     normed_t[...] = wide_normed.T.astype(low)
     own_ffn.wait()
     gather_step(0, 2, 0)
+    gather_step(1, 1, 0)
 
     first_row = (half * 8 + x * 2 + core) * TOK
 
@@ -290,7 +291,6 @@
     last_key = first_row + jnp.bitwise_and(lax.broadcasted_iota(jnp.int32, (STACK, 512), 0), TOK - 1)
 
     gather_step(0, 2, 1)
-    gather_step(1, 1, 0)
     for part in (2, 0, 1):
         settle(0, part)
         pass_on(part, 3, ring(spot[ORDERS[part][2]], 2))
@@ -319,6 +319,7 @@
         c, s = cosine[...], (-sine[...] if back else sine[...])
         return v1 * c - v2 * s, v2 * c + v1 * s
 
+    gather_step(1, 1, 1)
     settle_pairs(2)
     for where in groups:
         term = dot(weight_rows(where, pl.ds(128, 48)), normed_t[...])
@@ -348,13 +349,13 @@
     first = [key_copy(key_own, mine, 1 + way, neighbours[way]) for way in (0, 1)]
     kpairs.append(remote(key_own, mine, kpair_send.at[0], kpair_recv.at[0], sibling))
 
-    gather_step(1, 1, 1)
     settle_pairs(0)
     for where in groups:
         term = dot(weight_rows(where, pl.ds(0, 64)), normed_t[...])
         for i in range(4):
             rows_f32[pl.ds(60 * shard(where, i), 60)] = term[64 * i : 64 * i + 60]
 
+    gather_step(1, 2, 0, (0,))
     over.wait_recv()
     other = keys.at[1 - half, x, core]
     second = [key_copy(other, other, 3 + way, neighbours[way]) for way in (0, 1)]
@@ -371,8 +372,8 @@
         query[h] = jnp.concatenate([wide, apart], axis=0).T.astype(low)
         return carry
 
+    gather_step(1, 2, 0, (2,))
     lax.fori_loop(0, KVH, heads, 0)
-    gather_step(1, 2, 0, (0,))
 
     last = []
     for way, by in enumerate((1, -1)):
@@ -387,7 +388,7 @@
         if way == 1:
             last.append(key_copy(ref, ref, 6, neighbours[1]))
         pass_keys(ref)
-    gather_step(1, 2, 0, (1, 2))
+    gather_step(1, 2, 0, (1,))
     for h in (0, 1):
         last[h].wait_recv()
         pass_keys(keys.at[(half, 1 - half)[h], ring(x, 2), core])
@@ -696,18 +697,18 @@
         return key_terms.at[h, at, core]
 
     widen(d_query_t)
-    attn_grad(d_query_t[...], normed[...], 0, 64, 64)
-    share(0)
-    reduce_step(1, 1, 0)
     for h in (0, 1):
         copies[h].wait_recv()
         add(block(h, ring(x, 2)), key_pair.at[h, ring(x, 2)])
     far = [kg(block(way, ring(x, 2)), key_far.at[way], neighbours[way]) for way in (0, 1)]
+    attn_grad(d_query_t[...], normed[...], 0, 64, 64)
     for copy in copies[2:8]:
         copy.wait_recv()
+    share(0)
     for by in (1, 3, 0):
         for h in (0, 1):
             add(block(h, ring(x, by)), key_pair.at[h, ring(x, by)])
+    reduce_step(1, 1, 0)
     near = []
     for way, by in enumerate((1, -1)):
         far[way].wait_recv()

time: 160 us -> 159 us (level)
  no operation moved by 1% of the time
where the time goes in v3:
time: 159 us
  Pallas kernels  158 us (99%)
    pallas_call x1, Pallas kernels, run_layer(): pl.pallas_call(layer_kernel, out_shape=[jax.ShapeDtypeStruct((D, TOK), lo...  156 us

profile of v3, /device:TPU:0, one launch (start us, length us, event | category | flops | bytes accessed | tf_op | source)
XLA Modules:
  0.0 158.9 jit_solution(10546208983588998881)
XLA Ops:
  0.6 155.9 %layer.1 = (bf16[960,128]{1,0:T(8,128)(2,1)}, bf16[960,128]{1,0:T(8,128)(2,1)}, f32[60,120]{1,0:T(8,128)}, f32[20,120]{1,0:T(8,128)}, f32[20,120]{1,0:T(8,128)},...) custom-call(bf16[960,128]{1,0:T(8,128)(2,1)} %bitcast.30, ...), custom_call_target="tpu_custom_call" | custom-call | tf_op jit(solution)/shard_map/layer/pallas_call | solution.py:843
  156.6 2.2 %deliver.1 = (bf16[960,128]{1,0:T(8,128)(2,1)}, bf16[960,128]{1,0:T(8,128)(2,1)}, f32[60,120]{1,0:T(8,128)}, f32[20,120]{1,0:T(8,128)}, f32[20,120]{1,0:T(8,128)...) custom-call(bf16[960,128]{1,0:T(8,128)(2,1)} %get-tuple-element.32.r, ...), custom_call_target="tpu_custom_call" | custom-call | tf_op jit(solution)/shard_map/deliver/pallas_call | solution.py:938

commit v4 on v3

--- a/solution.py
+++ b/solution.py
@@ -709,19 +709,24 @@
         for h in (0, 1):
             add(block(h, ring(x, by)), key_pair.at[h, ring(x, by)])
     reduce_step(1, 1, 0)
-    near = []
     for way, by in enumerate((1, -1)):
         far[way].wait_recv()
         add(block(way, ring(x, by)), key_far.at[way])
-        near.append(kg(key_terms.at[:, ring(x, by), core], key_near.at[way], neighbours[way]))
-    reduce_step(1, 1, 1)
+    near = [
+        kg(block(h, ring(x, by)), key_near.at[way, h], neighbours[way])
+        for h in (1 - half, half)
+        for way, by in enumerate((1, -1))
+    ]
     reduce_step(0, 0, 1, (1,))
-    shared(0)
-    reduce_step(0, 0, 0, (0,))
-    for copy in near:
+    for copy in near[:2]:
         copy.wait_recv()
     add(block(1 - half, x), key_near.at[0, 1 - half], key_near.at[1, 1 - half])
     final = kg(block(1 - half, x), key_across, across)
+    reduce_step(1, 1, 1)
+    shared(0)
+    reduce_step(0, 0, 0, (0,))
+    for copy in near[2:]:
+        copy.wait_recv()
     add(block(half, x), key_near.at[0, half], key_near.at[1, half])
     reduce_step(1, 2, 0)
     norm_sum[pl.ds(0, TOK)] = jnp.zeros((TOK, WIDE), jnp.float32)
@@ -912,8 +917,8 @@
             dma((8,)),
             dma((4,)),
             dma((4,)),
-            dma((13,)),
-            dma((13,)),
+            dma((15,)),
+            dma((15,)),
             dma((2, 3, 3, 2, 3)),
             dma((2, 3, 3, 2, 3)),
             dma((3, 3)),

time: 159 us -> 164 us (1.031)
  Pallas kernels: 158 us -> 162 us
    pallas_call x1, Pallas kernels: 156 us -> 160 us  [run_layer(): pl.pallas_call(layer_kernel, out_shape=[jax.ShapeDtypeStruct((D, TOK), lo...]
where the time goes in v4:
time: 164 us; the launch traced here: 163 us
  Pallas kernels  162 us (99%)
    pallas_call x1, Pallas kernels, run_layer(): pl.pallas_call(layer_kernel, out_shape=[jax.ShapeDtypeStruct((D, TOK), lo...  160 us

profile of v4, /device:TPU:0, one launch (start us, length us, event | category | flops | bytes accessed | tf_op | source)
XLA Modules:
  0.0 163.0 jit_solution(11943161096927554744)
XLA Ops:
  0.6 160.0 %layer.1 = (bf16[960,128]{1,0:T(8,128)(2,1)}, bf16[960,128]{1,0:T(8,128)(2,1)}, f32[60,120]{1,0:T(8,128)}, f32[20,120]{1,0:T(8,128)}, f32[20,120]{1,0:T(8,128)},...) custom-call(bf16[960,128]{1,0:T(8,128)(2,1)} %bitcast.30, ...), custom_call_target="tpu_custom_call" | custom-call | tf_op jit(solution)/shard_map/layer/pallas_call | solution.py:848
  160.7 2.2 %deliver.1 = (bf16[960,128]{1,0:T(8,128)(2,1)}, bf16[960,128]{1,0:T(8,128)(2,1)}, f32[60,120]{1,0:T(8,128)}, f32[20,120]{1,0:T(8,128)}, f32[20,120]{1,0:T(8,128)...) custom-call(bf16[960,128]{1,0:T(8,128)(2,1)} %get-tuple-element.32.r, ...), custom_call_target="tpu_custom_call" | custom-call | tf_op jit(solution)/shard_map/deliver/pallas_call | solution.py:943

commit v5 on v4

--- a/solution.py
+++ b/solution.py
@@ -717,14 +717,14 @@
         for h in (1 - half, half)
         for way, by in enumerate((1, -1))
     ]
+    reduce_step(1, 1, 1)
     reduce_step(0, 0, 1, (1,))
+    shared(0)
+    reduce_step(0, 0, 0, (0,))
     for copy in near[:2]:
         copy.wait_recv()
     add(block(1 - half, x), key_near.at[0, 1 - half], key_near.at[1, 1 - half])
     final = kg(block(1 - half, x), key_across, across)
-    reduce_step(1, 1, 1)
-    shared(0)
-    reduce_step(0, 0, 0, (0,))
     for copy in near[2:]:
         copy.wait_recv()
     add(block(half, x), key_near.at[0, half], key_near.at[1, half])

time: 164 us -> 159 us (0.970)
  Pallas kernels: 162 us -> 158 us
    pallas_call x1, Pallas kernels: 160 us -> 156 us  [run_layer(): pl.pallas_call(layer_kernel, out_shape=[jax.ShapeDtypeStruct((D, TOK), lo...]
where the time goes in v5:
time: 159 us
  Pallas kernels  158 us (99%)
    pallas_call x1, Pallas kernels, run_layer(): pl.pallas_call(layer_kernel, out_shape=[jax.ShapeDtypeStruct((D, TOK), lo...  156 us

profile of v5, /device:TPU:0, one launch (start us, length us, event | category | flops | bytes accessed | tf_op | source)
XLA Modules:
  0.0 159.1 jit_solution(10565549756653857599)
XLA Ops:
  0.6 156.1 %layer.1 = (bf16[960,128]{1,0:T(8,128)(2,1)}, bf16[960,128]{1,0:T(8,128)(2,1)}, f32[60,120]{1,0:T(8,128)}, f32[20,120]{1,0:T(8,128)}, f32[20,120]{1,0:T(8,128)},...) custom-call(bf16[960,128]{1,0:T(8,128)(2,1)} %bitcast.30, ...), custom_call_target="tpu_custom_call" | custom-call | tf_op jit(solution)/shard_map/layer/pallas_call | solution.py:848
  156.8 2.2 %deliver.1 = (bf16[960,128]{1,0:T(8,128)(2,1)}, bf16[960,128]{1,0:T(8,128)(2,1)}, f32[60,120]{1,0:T(8,128)}, f32[20,120]{1,0:T(8,128)}, f32[20,120]{1,0:T(8,128)...) custom-call(bf16[960,128]{1,0:T(8,128)(2,1)} %get-tuple-element.32.r, ...), custom_call_target="tpu_custom_call" | custom-call | tf_op jit(solution)/shard_map/deliver/pallas_call | solution.py:943
